TPU v7x, 32 devices: a whole 2x2x4 slice. The times are simulated.
32 devices in a mesh: tile: 8 (over y, x, core), knot: 4 (over z).
Axes of the slice: x: 2, y: 2, z: 4, core: 2. Of those that a mesh axis runs over, the one named last changes fastest.
Arguments:
- images: float32 [8, 32, 65536], P('tile', 'knot'), may hold values from -6 to 6
- gradient: float32 [8, 32, 65536], P('tile', 'knot'), may hold values from -3 to 3
- shifts: int32 [8], P('tile'), may hold values from -4 to 4
- tile_blocks: int32 [8, 2], P('tile'), may hold values from 0 to 31, as said below
- intersections: int32 [8, 3, 8, 5], P('tile'), may hold values from 0 to 57344, as said below
- start_coefficients: float32 [32, 64], P(('tile', 'knot')), may hold values from -0.6 to 0.6
Outputs:
- coefficients: float32 [32, 64], P(('tile', 'knot'))
- warped: float32 [8, 32, 65536], P('tile', 'knot')
Inputs may be any that keep to these rules, and one draw needn't show every extreme that they name: intersections[s, d, m] holds the sending tile's index among the 1 tiles of owner s, its slab offset, the receiving tile's index among the tiles of owner s + d - 1, its slab offset, and a live flag; live slots of one sender and direction come first; no live slot points outside the owners; some owner receives 8 live slots from each of its three senders, and some sender fills 8 slots of a direction. `tile_blocks`: the blocks of a tile held by tile owner i are owned by tile owners i - 1, i or i + 1, block b being owned by device b div 1 in the order of tile and knot joined.
All inputs are finite; a program needn't handle non-finite values.
Results may differ from a plain program's by a relative error of at most 0.0003.
Values sent between devices are 32-bit elements; how exact they have to be, the bound alone decides.
A program may use at most 576 MiB of HBM per device.

v0:
```python
import jax
import jax.numpy as jnp
from jax import lax
from jax.sharding import PartitionSpec as P

SLAB = 8192
ITERS = 2


shift_step = 0.05
smooth_weight = 20.0
ridge_weight = 1.0


def extended(block, sides, width):
    for axis, dim in sides:
        count = lax.axis_size(axis)
        forward = [(i, i + 1) for i in range(count - 1)]
        backward = [(target, source) for source, target in forward]
        low = lax.ppermute(
            lax.slice_in_dim(block, block.shape[dim] - width, None, axis=dim), axis, forward
        )
        high = lax.ppermute(lax.slice_in_dim(block, 0, width, axis=dim), axis, backward)
        block = jnp.concatenate([low, block, high], axis=dim)
    return block


def from_behind(block, axis, distance):
    devices = range(lax.axis_size(axis))
    route = [(i - distance, i) for i in devices if i - distance in devices]
    return lax.ppermute(block, axis, route)


def spline_basis(plane, knots):
    place = jnp.arange(plane, dtype=jnp.float32) * ((knots - 3) / plane) + 1.0
    offset = place[None, :] - jnp.arange(knots, dtype=jnp.float32)[:, None]
    dist = jnp.abs(offset)
    inner = 2.0 / 3.0 - dist * dist + 0.5 * dist * dist * dist
    outer = (2.0 - dist) * (2.0 - dist) * (2.0 - dist) / 6.0
    return jnp.where(dist < 1.0, inner, jnp.where(dist < 2.0, outer, 0.0))


def smoothing(block):
    rows = jnp.arange(block - 2, dtype=jnp.int32)[:, None]
    cols = jnp.arange(block, dtype=jnp.int32)[None, :]
    second = (
        (cols == rows).astype(jnp.float32)
        - 2.0 * (cols == rows + 1).astype(jnp.float32)
        + (cols == rows + 2).astype(jnp.float32)
    )
    return jnp.dot(second.T, second, precision=lax.Precision.HIGHEST)


def block_update(normal, gradsum, coef, penalty):
    size = normal.shape[-1]
    system = normal + smooth_weight * penalty + ridge_weight * jnp.eye(size, dtype=jnp.float32)
    pull = jnp.einsum("kl,bl->bk", penalty, coef, precision=lax.Precision.HIGHEST)
    target = -(gradsum + smooth_weight * pull)
    factor = lax.linalg.cholesky(system)
    middle = lax.linalg.triangular_solve(factor, target[..., None], left_side=True, lower=True)
    update = lax.linalg.triangular_solve(
        factor, middle, left_side=True, lower=True, transpose_a=True
    )
    return coef + update[..., 0]


def per_device(images, gradient, shifts, tile_blocks, intersections, start_coefficients):
    tile_dev, depth, plane = images.shape
    kb_dev, block = start_coefficients.shape
    slab = SLAB
    basis = spline_basis(plane, 2 * block)
    penalty = smoothing(block)
    knot_count = lax.axis_size("knot")
    here = lax.axis_index("tile")
    links = intersections[0]
    cap = links.shape[1]
    flat = links.reshape(3 * cap, 5)
    rigid = shift_step * shifts.astype(jnp.float32)
    window = kb_dev * knot_count
    owned_tiles = jnp.arange(tile_dev, dtype=jnp.int32)

    def fetch(owned):
        column = lax.all_gather(owned, "knot", axis=0, tiled=True)
        table = extended(column, (("tile", 0),), window)
        first = (here - 1) * window
        wanted = tile_blocks.reshape(-1) - first
        select = (wanted[:, None] == jnp.arange(table.shape[0], dtype=jnp.int32)[None, :]).astype(
            jnp.float32
        )
        return jnp.dot(select, table, precision=lax.Precision.HIGHEST).reshape(tile_dev, 2 * block)

    def warp_tiles(owned):
        local = fetch(owned)
        field = jnp.dot(local, basis, precision=lax.Precision.HIGHEST) + rigid[:, None]
        return images + gradient * field[:, None, :]

    def cut(volume, which, start):
        return lax.dynamic_slice(volume, (which, 0, start), (1, depth, slab))[0]

    def cut_basis(start):
        return lax.dynamic_slice(basis, (0, start), (2 * block, slab))

    coef = start_coefficients
    for step in range(ITERS):
        tiles = warp_tiles(coef)
        slabs = jax.vmap(cut, (None, 0, 0))(tiles, flat[:, 0], flat[:, 1]).reshape(
            3, cap, depth, slab
        )
        labels = flat[:, 2:].astype(jnp.float32).reshape(3, cap, 3)
        below = from_behind((slabs[2], labels[2]), "tile", 1)
        above = from_behind((slabs[0], labels[0]), "tile", -1)
        arrived = jnp.stack([below[0], slabs[1], above[0]])
        arrived_labels = jnp.stack([below[1], labels[1], above[1]])
        arrived = arrived.reshape(3 * cap, depth, slab)
        arrived_labels = arrived_labels.reshape(3 * cap, 3)
        tile_a = arrived_labels[:, 0].astype(jnp.int32)
        off_a = arrived_labels[:, 1].astype(jnp.int32)
        alive = arrived_labels[:, 2]
        near = jax.vmap(cut, (None, 0, 0))(tiles, tile_a, off_a)
        slope = jax.vmap(cut, (None, 0, 0))(gradient, tile_a, off_a)
        misfit = (near - arrived) * alive[:, None, None]
        weight = jnp.sum(slope * slope, axis=1) * alive[:, None]
        project = jnp.sum(slope * misfit, axis=1)
        piece = jax.vmap(cut_basis)(off_a).reshape(3 * cap, 2, block, slab)
        normals = jnp.einsum(
            "pnks,pnls->pnkl",
            piece * weight[:, None, None, :],
            piece,
            precision=lax.Precision.HIGHEST,
        )
        grads = jnp.einsum("pnks,ps->pnk", piece, project, precision=lax.Precision.HIGHEST)
        pick = (tile_a[:, None] == owned_tiles[None, :]).astype(jnp.int32)
        dest = jnp.sum(pick[:, :, None] * tile_blocks[None, :, :], axis=1).reshape(-1)
        normals = normals.reshape(-1, block, block)
        grads = grads.reshape(-1, block)
        rows = dest - (here - 1) * window
        select = (jnp.arange(3 * window, dtype=jnp.int32)[:, None] == rows[None, :]).astype(
            jnp.float32
        )
        normal_term = jnp.einsum(
            "bq,qkl->bkl", select, normals, precision=lax.Precision.HIGHEST
        ).reshape(3, knot_count, kb_dev, block, block)
        grad_term = jnp.dot(select, grads, precision=lax.Precision.HIGHEST).reshape(
            3, knot_count, kb_dev, block
        )
        column_normal, column_grad = (
            lax.psum_scatter(normal_term, "knot", scatter_dimension=1, tiled=True),
            lax.psum_scatter(grad_term, "knot", scatter_dimension=1, tiled=True),
        )
        upper = from_behind((column_normal[0], column_grad[0]), "tile", -1)
        lower = from_behind((column_normal[2], column_grad[2]), "tile", 1)
        normal_sum = (column_normal[1] + upper[0] + lower[0]).reshape(kb_dev, block, block)
        grad_sum = (column_grad[1] + upper[1] + lower[1]).reshape(kb_dev, block)
        coef = block_update(normal_sum, grad_sum, coef, penalty)
    warped = warp_tiles(coef)
    return (coef, warped)


def solution(mesh):
    placed = (
        P("tile", "knot", None),
        P("tile", "knot", None),
        P("tile"),
        P("tile", None),
        P("tile", None, None, None),
        P(("tile", "knot"), None),
    )
    return jax.shard_map(
        per_device,
        mesh=mesh,
        in_specs=placed,
        out_specs=(P(("tile", "knot"), None), P("tile", "knot", None)),
        check_vma=False,
    )
```

profile of v0, /device:TPU:0, one launch (start us, length us, event | category | flops | bytes accessed | tf_op | source)
XLA Modules:
  0.0 1173.4 jit_solution(1429191343413483131)
XLA Ops:
  7.2 12.7 %all-gather = f32[4,1,64]{2,1,0:T(1,128)S(1)} all-gather(f32[1,1,64]{2,1,0:T(1,128)} %bitcast.325), channel_id=1, replica_groups=mesh['tile'=8,'knot'=4] {'knot'}, dimensions={0}, use_global_device_ids=true | all-gather | bytes 1280 | tf_op jit(solution)/shard_map/all_gather | solution.py:83
  32.6 19.4 %fusion.4 = f32[128,65536]{1,0:T(8,128)} fusion(f32[65536]{0:T(1024)S(1)} %multiply_add_fusion.3), kind=kLoop, calls=%fused_computation.18 | loop fusion | flops 134217728 | bytes 33816576 | tf_op jit(solution)/shard_map/jit(_where)/select_n | solution.py:40
  53.6 155.9 %while.6 = (s32[]{:T(128)}, f32[128,65536]{1,0:T(8,128)}, s32[24,2]{0,1:T(2,128)S(1)}, f32[24,128,8192]{2,1,0:T(8,128)}, s32[]{:T(128)}) while((s32[]{:T(128)}, f32[128,65536]{1,0:T(8,128)}, s32[24,2]{0,1:T(2,128)S(1)}, f32[24,128,8192]{2,1,0:T(8,128)}, s32[]{:T(128)}) %tuple.92), condition=%wide.while_cond, body=%wide.while_body.sunk | while | flops 2 | bytes 8389221 | solution.py:101
  60.6 5.9 bitcast_dynamic-update-slice_fusion.12
  86.6 5.9 bitcast_dynamic-update-slice_fusion.12
  93.1 5.9 bitcast_dynamic-update-slice_fusion.12
  106.0 6.0 bitcast_dynamic-update-slice_fusion.12
  112.6 5.9 bitcast_dynamic-update-slice_fusion.12
  132.1 6.0 bitcast_dynamic-update-slice_fusion.12
  138.6 5.9 bitcast_dynamic-update-slice_fusion.12
  158.1 5.9 bitcast_dynamic-update-slice_fusion.12
  171.1 5.9 bitcast_dynamic-update-slice_fusion.12
  184.0 5.9 bitcast_dynamic-update-slice_fusion.12
  203.5 5.9 bitcast_dynamic-update-slice_fusion.12
  212.7 49.9 %while.7 = (s32[]{:T(128)}, f32[1,8,65536]{2,1,0:T(8,128)S(1)}, s32[24,3]{0,1:T(4,128)S(1)}, f32[24,1,8,8192]{3,2,1,0:T(8,128)}, s32[]{:T(128)}) while((s32[]{:T(128)}, f32[1,8,65536]{2,1,0:T(8,128)S(1)}, s32[24,3]{0,1:T(4,128)S(1)}, f32[24,1,8,8192]{3,2,1,0:T(8,128)}, s32[]{:T(128)}) %tuple.112), condition=%wide.while_cond.1, body=%wide.while_body.1.sunk | while | flops 2 | bytes 524909 | solution.py:98
  263.0 33.4 %fusion.14 = f32[1,65536]{1,0:T(1,128)S(1)} fusion(f32[128,1]{0,1:T(1,128)S(1)} %reshape.516, f32[65536]{0:T(1024)S(1)} %multiply_add_fusion.3), kind=kOutput, calls=%fused_computation.27 | convolution fusion | flops 234881024 | bytes 524800 | tf_op jit(solution)/shard_map/dot_general | solution.py:94
  301.5 69.4 %while.9 = (s32[]{:T(128)}, f32[1,8,65536]{2,1,0:T(8,128)}, s32[24,3]{0,1:T(4,128)S(1)}, f32[24,1,8,8192]{3,2,1,0:T(8,128)}, s32[]{:T(128)}) while((s32[]{:T(128)}, f32[1,8,65536]{2,1,0:T(8,128)}, s32[24,3]{0,1:T(4,128)S(1)}, f32[24,1,8,8192]{3,2,1,0:T(8,128)}, s32[]{:T(128)}) %tuple.95), condition=%wide.while_cond.3, body=%wide.while_body.3.sunk | while | flops 2 | bytes 524909 | solution.py:98
  385.6 74.0 %while.8 = (s32[]{:T(128)}, f32[1,8,65536]{2,1,0:T(8,128)}, s32[24,3]{0,1:T(4,128)S(1)}, f32[24,1,8,8192]{3,2,1,0:T(8,128)}, s32[]{:T(128)}) while((s32[]{:T(128)}, f32[1,8,65536]{2,1,0:T(8,128)}, s32[24,3]{0,1:T(4,128)S(1)}, f32[24,1,8,8192]{3,2,1,0:T(8,128)}, s32[]{:T(128)}) %tuple.115), condition=%wide.while_cond.2, body=%wide.while_body.2.sunk | while | flops 2 | bytes 524909 | solution.py:98
  466.7 12.7 %fusion.21 = (f32[24,8192]{1,0:T(8,128)}, f32[24,8192]{1,0:T(8,128)}) fusion(f32[3,8,8,8192]{3,2,1,0:T(8,128)} %pad_maximum_fusion, f32[24,1,8,8192]{3,2,1,0:T(8,128)} %get-tuple-element.28, f32[24,1,8,8192]{3,2,1,0:T(8,128)} %get-tuple-element.20, f32[24]{0:T(128)S(1)} %slice_bitcast_fusion.7), kind=kLoop, calls=%fused_computation.37 | loop fusion | flops 9043968 | bytes 20447328 | tf_op jit(solution)/shard_map/reduce_sum | solution.py:123
  480.7 102.3 %fusion = f32[24,2,64,64]{3,2,1,0:T(8,128)} fusion(f32[24,2,64,8192]{3,2,1,0:T(8,128)} %bitcast.7, f32[24,8192]{1,0:T(8,128)S(1)} %broadcast_multiply_fusion), kind=kOutput, calls=%fused_computation.12 | convolution fusion | flops 19352518656 | bytes 102236160 | tf_op jit(solution)/shard_map/pnks,pnls->pnkl/dot_general | solution.py:125
  586.9 121.6 %fusion.33 = f32[24,1,2,64]{3,1,2,0:T(1,128)S(1)} fusion(f32[24,2,64,8192]{3,2,1,0:T(8,128)} %bitcast.7, f32[24,8192,1,1]{1,0,2,3:T(8,128)} %bitcast.316), kind=kOutput, calls=%fused_computation.65 | convolution fusion | flops 301989888 | bytes 101462016 | tf_op jit(solution)/shard_map/pnks,ps->pnk/dot_general | solution.py:131
  708.7 8.5 all-reduce.2
  742.2 9.4 all-gather.1
  757.1 33.3 %fusion.12 = f32[1,65536]{1,0:T(1,128)S(1)} fusion(f32[128,1]{0,1:T(1,128)S(1)} %reshape.527, f32[65536]{0:T(1024)S(1)} %multiply_add_fusion.3), kind=kOutput, calls=%fused_computation.26 | convolution fusion | flops 234881024 | bytes 524800 | tf_op jit(solution)/shard_map/dot_general | solution.py:94
  795.4 75.0 %while.11 = (s32[]{:T(128)}, f32[1,8,65536]{2,1,0:T(8,128)}, s32[24,3]{0,1:T(4,128)S(1)}, f32[24,1,8,8192]{3,2,1,0:T(8,128)}, s32[]{:T(128)}) while((s32[]{:T(128)}, f32[1,8,65536]{2,1,0:T(8,128)}, s32[24,3]{0,1:T(4,128)S(1)}, f32[24,1,8,8192]{3,2,1,0:T(8,128)}, s32[]{:T(128)}) %tuple.117), condition=%wide.while_cond.5, body=%wide.while_body.5.sunk | while | flops 2 | bytes 524909 | solution.py:98
  876.2 7.4 collective-permute-start.12
  886.9 72.8 %while.10 = (s32[]{:T(128)}, f32[1,8,65536]{2,1,0:T(8,128)}, s32[24,3]{0,1:T(4,128)S(1)}, f32[24,1,8,8192]{3,2,1,0:T(8,128)}, s32[]{:T(128)}) while((s32[]{:T(128)}, f32[1,8,65536]{2,1,0:T(8,128)}, s32[24,3]{0,1:T(4,128)S(1)}, f32[24,1,8,8192]{3,2,1,0:T(8,128)}, s32[]{:T(128)}) %tuple.116), condition=%wide.while_cond.4, body=%wide.while_body.4.sunk | while | flops 2 | bytes 524909 | solution.py:98
  966.8 9.7 fusion.18
  976.5 122.1 %fusion.31 = f32[24,1,2,64]{3,1,2,0:T(1,128)S(1)} fusion(f32[24,2,64,8192]{3,2,1,0:T(8,128)} %bitcast.7, f32[24,8192,1,1]{1,0,2,3:T(8,128)S(1)} %bitcast.317), kind=kOutput, calls=%fused_computation.63 | convolution fusion | flops 301989888 | bytes 101462016 | tf_op jit(solution)/shard_map/pnks,ps->pnk/dot_general | solution.py:131
  1098.9 8.6 all-reduce.3
  1116.6 9.5 all-gather.2
  1131.6 32.9 %fusion.10 = f32[1,65536]{1,0:T(1,128)S(1)} fusion(f32[128,1]{0,1:T(1,128)S(1)} %reshape.538, f32[65536]{0:T(1024)S(1)} %multiply_add_fusion.3), kind=kOutput, calls=%fused_computation.25 | convolution fusion | flops 234881024 | bytes 524800 | tf_op jit(solution)/shard_map/dot_general | solution.py:94
  (551 shorter events, 548.6 us)
Async XLA Ops:
  7.2 710.1 %all-reduce.6.cloned.1.call-start = ((), (), s32[]{:S(2)}) async-start(), calls=%async_computation | async-start | bytes 786432
  19.9 242.8 %collective-permute-start.5 = (f32[4,64]{1,0:T(4,128)S(1)}, f32[4,64]{1,0:T(4,128)S(1)}, u32[]{:S(2)}, u32[]{:S(2)}) collective-permute-start(f32[4,64]{1,0:T(4,128)S(1)} %bitcast.327), channel_id=1, source_target_pairs={{4,0},{8,4},{12,8},{16,12},{20,16},{24,20},{28,24},{5,1},{9,5},{13... | collective-permute-start | bytes 3080 | tf_op jit(solution)/shard_map/ppermute | solution.py:23
  21.2 241.5 %collective-permute-start.4 = (f32[4,64]{1,0:T(4,128)S(1)}, f32[4,64]{1,0:T(4,128)S(1)}, u32[]{:S(2)}, u32[]{:S(2)}) collective-permute-start(f32[4,64]{1,0:T(4,128)S(1)} %bitcast.328), channel_id=1, source_target_pairs={{0,4},{4,8},{8,12},{12,16},{16,20},{20,24},{24,28},{1,5},{5,9},{9,... | collective-permute-start | bytes 3080 | tf_op jit(solution)/shard_map/ppermute | solution.py:20
  25.1 28.3 %collective-permute-start.1 = (f32[8,3]{0,1:T(4,128)S(1)}, f32[8,3]{0,1:T(4,128)S(1)}, u32[]{:S(2)}, u32[]{:S(2)}) collective-permute-start(f32[8,3]{0,1:T(4,128)S(1)} %get-tuple-element.118), channel_id=1, source_target_pairs={{4,0},{8,4},{12,8},{16,12},{20,16},{24,20},{28,24},{5,1},{9,5},{13... | collective-permute-start | bytes 296 | tf_op jit(solution)/shard_map/ppermute | solution.py:31
  26.4 27.0 %collective-permute-start = (f32[8,3]{0,1:T(4,128)S(1)}, f32[8,3]{0,1:T(4,128)S(1)}, u32[]{:S(2)}, u32[]{:S(2)}) collective-permute-start(f32[8,3]{0,1:T(4,128)S(1)} %get-tuple-element.117), channel_id=1, source_target_pairs={{0,4},{4,8},{8,12},{12,16},{16,20},{20,24},{24,28},{1,5},{5,9},{9,... | collective-permute-start | bytes 296 | tf_op jit(solution)/shard_map/ppermute | solution.py:31
  30.5 21.5 %copy-start.4 = (f32[64,64]{1,0:T(8,128)}, f32[64,64]{1,0:T(8,128)S(1)}, u32[]{:S(2)}) copy-start(f32[64,64]{1,0:T(8,128)S(1)} %fusion.46) | copy-start | bytes 49156
  32.6 20.1 %copy-start.10 = (s32[1,2]{1,0:T(1,128)S(1)}, s32[1,2]{1,0:T(1,128)}, u32[]{:S(2)}) copy-start(s32[1,2]{1,0:T(1,128)} %param.14) | copy-start | bytes 28
  32.6 20.1 %copy-start.11 = (u32[32]{0:T(128)S(1)}, u32[32]{0:T(128)}, u32[]{:S(2)}) copy-start(u32[32]{0:T(128)} %constant.171) | copy-start | bytes 388
  53.5 159.2 %copy-start = (f32[1,8,65536]{2,1,0:T(8,128)S(1)}, f32[1,8,65536]{2,1,0:T(8,128)}, u32[]{:S(2)}) copy-start(f32[1,8,65536]{2,1,0:T(8,128)} %param.12) | copy-start | bytes 6291460
  263.0 33.4 %copy-start.1 = (f32[1,8,65536]{2,1,0:T(8,128)S(1)}, f32[1,8,65536]{2,1,0:T(8,128)}, u32[]{:S(2)}) copy-start(f32[1,8,65536]{2,1,0:T(8,128)} %param.11) | copy-start | bytes 6291460
  375.4 85.9 %collective-permute-start.7 = (f32[8,8,8192]{2,1,0:T(8,128)}, f32[8,8,8192]{2,1,0:T(8,128)}, u32[]{:S(2)}, u32[]{:S(2)}) collective-permute-start(f32[8,8,8192]{2,1,0:T(8,128)} %get-tuple-element.106), channel_id=1, source_target_pairs={{4,0},{8,4},{12,8},{16,12},{20,16},{24,20},{28,24},{5,1},{9,5},{13... | collective-permute-start | bytes 6291464 | tf_op jit(solution)/shard_map/ppermute | solution.py:31
  376.7 84.7 %collective-permute-start.6 = (f32[8,8,8192]{2,1,0:T(8,128)}, f32[8,8,8192]{2,1,0:T(8,128)}, u32[]{:S(2)}, u32[]{:S(2)}) collective-permute-start(f32[8,8,8192]{2,1,0:T(8,128)} %get-tuple-element.105), channel_id=1, source_target_pairs={{0,4},{4,8},{8,12},{12,16},{16,20},{20,24},{24,28},{1,5},{5,9},{9,... | collective-permute-start | bytes 6291464 | tf_op jit(solution)/shard_map/ppermute | solution.py:31
  586.9 140.8 %copy-start.6 = (f32[64,64]{0,1:T(8,128)S(1)}, f32[64,64]{0,1:T(8,128)}, u32[]{:S(2)}) copy-start(f32[64,64]{0,1:T(8,128)} %copy.32) | copy-start | bytes 49156
  586.9 154.4 %copy-start.8 = (f32[64]{0:T(128)S(1)}, f32[64]{0:T(128)}, u32[]{:S(2)}) copy-start(f32[64]{0:T(128)} %fusion.30) | copy-start | bytes 772
  586.9 155.2 %copy-start.7 = (f32[1,64]{1,0:T(1,128)S(1)}, f32[1,64]{1,0:T(1,128)}, u32[]{:S(2)}) copy-start(f32[1,64]{1,0:T(1,128)} %param.16) | copy-start | bytes 772
  718.7 9.0 collective-permute-start.3
  720.0 7.7 collective-permute-start.2
  721.9 19.4 %collective-permute-start.9 = (f32[1,1,64]{2,1,0:T(1,128)S(1)}, f32[1,1,64]{2,1,0:T(1,128)S(1)}, u32[]{:S(2)}, u32[]{:S(2)}) collective-permute-start(f32[1,1,64]{2,1,0:T(1,128)S(1)} %get-tuple-element.112), channel_id=1, source_target_pairs={{0,4},{4,8},{8,12},{12,16},{16,20},{20,24},{24,28},{1,5},{5,9},{9,... | collective-permute-start | bytes 776 | tf_op jit(solution)/shard_map/ppermute | solution.py:31
  726.3 14.9 %collective-permute-start.8 = (f32[1,1,64]{2,1,0:T(1,128)S(1)}, f32[1,1,64]{2,1,0:T(1,128)S(1)}, u32[]{:S(2)}, u32[]{:S(2)}) collective-permute-start(f32[1,1,64]{2,1,0:T(1,128)S(1)} %get-tuple-element.111), channel_id=1, source_target_pairs={{4,0},{8,4},{12,8},{16,12},{20,16},{24,20},{28,24},{5,1},{9,5},{13... | collective-permute-start | bytes 776 | tf_op jit(solution)/shard_map/ppermute | solution.py:31
  751.7 4.3 collective-permute-start.11
  753.0 3.8 collective-permute-start.10
  757.1 33.3 %copy-start.2 = (f32[1,8,65536]{2,1,0:T(8,128)S(1)}, f32[1,8,65536]{2,1,0:T(8,128)}, u32[]{:S(2)}) copy-start(f32[1,8,65536]{2,1,0:T(8,128)} %param.11) | copy-start | bytes 6291460
  874.9 86.4 %collective-permute-start.13 = (f32[8,8,8192]{2,1,0:T(8,128)}, f32[8,8,8192]{2,1,0:T(8,128)}, u32[]{:S(2)}, u32[]{:S(2)}) collective-permute-start(f32[8,8,8192]{2,1,0:T(8,128)} %get-tuple-element.104), channel_id=1, source_target_pairs={{4,0},{8,4},{12,8},{16,12},{20,16},{24,20},{28,24},{5,1},{9,5},{13... | collective-permute-start | bytes 6291464 | tf_op jit(solution)/shard_map/ppermute | solution.py:31
  876.2 85.2 %collective-permute-start.12 = (f32[8,8,8192]{2,1,0:T(8,128)}, f32[8,8,8192]{2,1,0:T(8,128)}, u32[]{:S(2)}, u32[]{:S(2)}) collective-permute-start(f32[8,8,8192]{2,1,0:T(8,128)} %get-tuple-element.103), channel_id=1, source_target_pairs={{0,4},{4,8},{8,12},{12,16},{16,20},{20,24},{24,28},{1,5},{5,9},{9,... | collective-permute-start | bytes 6291464 | tf_op jit(solution)/shard_map/ppermute | solution.py:31
  976.5 134.2 %copy-start.5 = (f32[64,64]{1,0:T(8,128)S(1)}, f32[64,64]{1,0:T(8,128)}, u32[]{:S(2)}) copy-start(f32[64,64]{1,0:T(8,128)} %copy-done.4) | copy-start | bytes 49156
  1108.2 2.8 collective-permute-start.15
  1109.5 6.2 collective-permute-start.14
  1116.6 47.8 %copy-start.9 = (f32[1,64]{1,0:T(1,128)}, f32[1,64]{1,0:T(1,128)S(1)}, u32[]{:S(2)}) copy-start(f32[1,64]{1,0:T(1,128)S(1)} %convolution_add_fusion) | copy-start | bytes 772
  1126.2 4.3 collective-permute-start.17
  1127.4 3.8 collective-permute-start.16
  1131.5 32.9 %copy-start.3 = (f32[1,8,65536]{2,1,0:T(8,128)S(1)}, f32[1,8,65536]{2,1,0:T(8,128)}, u32[]{:S(2)}) copy-start(f32[1,8,65536]{2,1,0:T(8,128)} %param.11) | copy-start | bytes 6291460
Sparse Core Ops, SparseCore 0:
  587.0 36.1 all-reduce.5
where the time goes:
time: 1190 us; the launch traced here: 1170 us
  local copies, waits for them, and re-layouts  532 us (45%)
  matrix products  453 us (38%)
  other arithmetic  72.7 us (6%)
  blocking collectives  48.8 us (4%)
  starting transfers between devices  44.3 us (4%)
  between operations  15.7 us (1%)
    gather x432, local copies, waits for them, and re-layouts  497 us
    dot_general x2, matrix products, per_device(): jnp.einsum('pnks,ps->pnk', piece, project, precision=lax.Precision.HIGHEST)  244 us
    dot_general x1, matrix products, per_device(): jnp.einsum('pnks,pnls->pnkl', piece * weight[:, None, None, :], piece, pr...  102 us
    dot_general x3, matrix products, warp_tiles(): jnp.dot(local, basis, precision=lax.Precision.HIGHEST) + rigid[:, None]  99.5 us
    all_gather x3, blocking collectives, fetch(): column = lax.all_gather(owned, 'knot', axis=0, tiled=True)  31.7 us
    ppermute x12, starting transfers between devices, from_behind(): return lax.ppermute(block, axis, route)  31.3 us
  transfers between devices with their start and end apart: 19, of which 3 were waited for; matrix products, arithmetic and copies ran while one was open for 45% of the time, Pallas kernels for 0%

commit v1 on v0

v1 whole, which is shorter than its diff:
```python
import functools

import jax
import jax.numpy as jnp
import numpy as np
from jax import lax
from jax.experimental import pallas as pl
from jax.experimental.pallas import tpu as pltpu
from jax.sharding import PartitionSpec as P

SLAB = 8192
ITERS = 2
LANES = 128
SUB = 8
GROUP = SUB * LANES
FRONT = 8
BACK = 16
WINDOW = 6
BAND = 4
SPAN = SLAB // GROUP + 1

shift_step = 0.05
smooth_weight = 20.0
ridge_weight = 1.0
HIGHEST = lax.Precision.HIGHEST
MESH = pl.DeviceIdType.MESH
VMEM = pl.BlockSpec(memory_space=pltpu.VMEM)
SMEM = pl.BlockSpec(memory_space=pltpu.SMEM)
PARAMS = pltpu.CompilerParams(vmem_limit_bytes=48 * 1024 * 1024)


def f32(*shape):
    return jax.ShapeDtypeStruct(shape, jnp.float32)


def smoothing(block):
    second = np.zeros((block - 2, block), np.float32)
    for row in range(block - 2):
        second[row, row : row + 3] = (1.0, -2.0, 1.0)
    return second.T @ second


def cols_dot(left, right):
    return lax.dot_general(
        left, right, (((0,), (0,)), ((), ())), precision=HIGHEST,
        preferred_element_type=jnp.float32,
    )


def lanes_dot(left, right):
    return lax.dot_general(
        left, right, (((1,), (1,)), ((), ())), precision=HIGHEST,
        preferred_element_type=jnp.float32,
    )


def grid_iota():
    sub = lax.broadcasted_iota(jnp.int32, (SUB, LANES), 0)
    lane = lax.broadcasted_iota(jnp.int32, (SUB, LANES), 1)
    return sub, lane


def first_knot(group, plane, knots):
    return lax.div(group * (GROUP * (knots - 3)), plane)


def clear(ref):
    ref[...] = jnp.zeros(ref.shape, ref.dtype)


def to_planes(depth, groups, flat_ref, out_ref):
    rows = groups * SUB
    for z in range(depth):
        out_ref[z, 0:FRONT, :] = jnp.zeros((FRONT, LANES), jnp.float32)
        out_ref[z, FRONT + rows : FRONT + rows + BACK, :] = jnp.zeros((BACK, LANES), jnp.float32)

    def body(group, _):
        for z in range(depth):
            out_ref[z, pl.ds(pl.multiple_of(FRONT + group * SUB, SUB), SUB), :] = flat_ref[
                pl.ds(group * (SUB * depth) + z, SUB, stride=depth), :
            ]
        return 0

    lax.fori_loop(0, groups, body, 0)


def lane_sums(acc, knots):
    partial = jnp.sum(acc[0:knots], axis=1)
    return lanes_dot(jnp.ones((SUB, LANES), jnp.float32), partial)[0:1, :]


def own_kernel(
    depth, plane, knots, table, image, slope, basis, weight, pull, bands, image_planes,
    slope_planes, count, acc,
):
    groups = plane // GROUP
    sub, lane = grid_iota()
    place0 = sub * LANES + lane
    to_planes(depth, groups, image, image_planes)
    to_planes(depth, groups, slope, slope_planes)
    clear(count)
    clear(acc)

    def add_pair(pair, _):
        off = table[pair, 3]
        live = table[pair, 4].astype(jnp.float32)
        row = lax.shift_right_logical(off, 10) * SUB
        low = off & (GROUP - 1)
        for i in range(SPAN):
            at = pl.ds(pl.multiple_of(FRONT + row + i * SUB, SUB), SUB)
            s = place0 + (i * GROUP - low)
            count[at, :] += jnp.where((s >= 0) & (s < SLAB), live, 0.0)
        return 0

    lax.fori_loop(0, table.shape[0], add_pair, 0)

    def body(group, _):
        at = pl.ds(pl.multiple_of(FRONT + group * SUB, SUB), SUB)
        squares = jnp.zeros((SUB, LANES), jnp.float32)
        cross = jnp.zeros((SUB, LANES), jnp.float32)
        for z in range(depth):
            g = slope_planes[z, at, :]
            squares += g * g
            cross += g * image_planes[z, at, :]
        w = squares * count[at, :]
        here = pl.ds(pl.multiple_of(group * SUB, SUB), SUB)
        weight[here, :] = w
        pull[here, :] = cross * count[at, :]
        first = first_knot(group, plane, knots)
        place = (place0 + group * GROUP).astype(jnp.float32) * ((knots - 3) / plane) + 1.0
        parts = []
        for i in range(WINDOW):
            dist = jnp.abs(place - (first + i).astype(jnp.float32))
            inner = 2.0 / 3.0 - dist * dist + 0.5 * dist * dist * dist
            outer = (2.0 - dist) * (2.0 - dist) * (2.0 - dist) * (1.0 / 6.0)
            value = jnp.where(dist < 1.0, inner, jnp.where(dist < 2.0, outer, 0.0))
            basis[group * WINDOW + i] = value
            parts.append(value)
        for i in range(WINDOW):
            scaled = parts[i] * w
            for d in range(min(BAND, WINDOW - i)):
                acc[d, first + i] += scaled * parts[i + d]
        return 0

    lax.fori_loop(0, groups, body, 0)
    bands[...] = jnp.concatenate(
        [lane_sums(acc.at[d], knots) for d in range(BAND)]
        + [jnp.zeros((SUB - BAND, LANES), jnp.float32)],
        axis=0,
    )


def pair_place(table, pair):
    low = table[pair, 1] & (GROUP - 1)
    start = table[pair, 1] - low
    shift = table[pair, 3] - low
    row_b = pl.multiple_of(FRONT + lax.shift_right_logical(start, 7), SUB)
    row_a = FRONT + lax.shift_right_arithmetic(shift, 7)
    return low, row_b, row_a, shift & (LANES - 1)


def pair_kernel(depth, plane, table, far_slope, image_planes, slope_planes, image_sum, slope_sum, far):
    sub, lane = grid_iota()
    place0 = sub * LANES + lane
    to_planes(depth, plane // GROUP, far_slope, far)

    def body(pair, _):
        low, row_b, row_a, turn = pair_place(table, pair)
        live = table[pair, 4].astype(jnp.float32)
        back = (LANES - turn) & (LANES - 1)
        keep = lane >= turn
        for i in range(SPAN):
            at = pl.ds(pl.multiple_of(row_b + i * SUB, SUB), SUB)
            c = jnp.zeros((SUB, LANES), jnp.float32)
            d = jnp.zeros((SUB, LANES), jnp.float32)
            for z in range(depth):
                a = jnp.where(
                    keep,
                    far[z, pl.ds(row_a + i * SUB, SUB), :],
                    far[z, pl.ds(row_a + i * SUB + 1, SUB), :],
                )
                a = pltpu.roll(a, back, 1)
                c += a * image_planes[z, at, :]
                d += a * slope_planes[z, at, :]
            s = place0 + (i * GROUP - low)
            inside = (s >= 0) & (s < SLAB)
            image_sum[pair, pl.ds(i * SUB, SUB), :] = jnp.where(inside, c * live, 0.0)
            slope_sum[pair, pl.ds(i * SUB, SUB), :] = jnp.where(inside, d * live, 0.0)
        return 0

    lax.fori_loop(0, table.shape[0], body, 0)


def project_kernel(
    plane, knots, cap, table, coef, rigid, basis, weight, pull, c0, d0, c1, d1, c2, d2,
    grads, field, landed, acc,
):
    groups = plane // GROUP
    rows = plane // LANES
    sub, lane = grid_iota()
    field[0:FRONT, :] = jnp.zeros((FRONT, LANES), jnp.float32)
    field[FRONT + rows : FRONT + rows + BACK, :] = jnp.zeros((BACK, LANES), jnp.float32)
    clear(landed)
    clear(acc)
    base = shift_step * rigid[0].astype(jnp.float32)

    def fill(group, _):
        first = first_knot(group, plane, knots)
        value = jnp.zeros((SUB, LANES), jnp.float32)
        for i in range(WINDOW):
            value += coef[first + i] * basis[group * WINDOW + i]
        field[pl.ds(pl.multiple_of(FRONT + group * SUB, SUB), SUB), :] = value + base
        return 0

    lax.fori_loop(0, groups, fill, 0)

    for side, (c, d) in enumerate(((c0, d0), (c1, d1), (c2, d2))):

        def body(pair, _):
            low, row_b, row_a, turn = pair_place(table, side * cap + pair)
            keep = lane >= turn
            for i in range(SPAN):
                at = pl.ds(pl.multiple_of(row_b + i * SUB, SUB), SUB)
                here = pl.ds(i * SUB, SUB)
                term = c[pair, here, :] + field[at, :] * d[pair, here, :]
                term = pltpu.roll(term, turn, 1)
                landed[side, pl.ds(row_a + i * SUB, SUB), :] += jnp.where(keep, term, 0.0)
                landed[side, pl.ds(row_a + i * SUB + 1, SUB), :] += jnp.where(keep, 0.0, term)
            return 0

        lax.fori_loop(0, cap, body, 0)

    def gather(group, _):
        first = first_knot(group, plane, knots)
        at = pl.ds(pl.multiple_of(FRONT + group * SUB, SUB), SUB)
        here = pl.ds(pl.multiple_of(group * SUB, SUB), SUB)
        own = pull[here, :] + weight[here, :] * field[at, :] - landed[1, at, :]
        values = (own, -landed[0, at, :], -landed[2, at, :])
        for i in range(WINDOW):
            b = basis[group * WINDOW + i]
            for q in range(3):
                acc[q, first + i] += b * values[q]
        return 0

    lax.fori_loop(0, groups, gather, 0)
    grads[...] = jnp.concatenate(
        [lane_sums(acc.at[q], knots) for q in range(3)]
        + [jnp.zeros((SUB - 3, LANES), jnp.float32)],
        axis=0,
    )


def share_kernel(knot_count, total, mine, out, held, send_sem, recv_sem):
    me = lax.axis_index("tile") * knot_count + lax.axis_index("knot")

    def peer(step):
        other = lax.rem(me + step, total)
        return other, (lax.div(other, knot_count), lax.rem(other, knot_count))

    barrier = pltpu.get_barrier_semaphore()

    def greet(step, _):
        pl.semaphore_signal(barrier, inc=1, device_id=peer(step)[1], device_id_type=MESH)
        return 0

    lax.fori_loop(1, total, greet, 0)
    pl.semaphore_wait(barrier, total - 1)

    def copy(step, slot):
        return pltpu.make_async_remote_copy(
            src_ref=mine,
            dst_ref=held.at[slot],
            send_sem=send_sem.at[step],
            recv_sem=recv_sem.at[slot],
            device_id=peer(step)[1],
            device_id_type=MESH,
        )

    def send(step, _):
        copy(step, me).start()
        return 0

    lax.fori_loop(1, total, send, 0)
    held[me] = mine[...]

    def arrive(step, _):
        copy(step, peer(step)[0]).wait_recv()
        return 0

    lax.fori_loop(1, total, arrive, 0)
    out[...] = held[...]

    def sent(step, _):
        copy(step, me).wait_send()
        return 0

    lax.fori_loop(1, total, sent, 0)


def local_rows(index, coef):
    sub = lax.broadcasted_iota(jnp.int32, (SUB, LANES), 0)
    lane = lax.broadcasted_iota(jnp.int32, (SUB, LANES), 1)
    want = jnp.where(sub == 0, index[0], jnp.where(sub == 1, index[1], index[2]))
    hot = ((lane == want) & (sub < 3)).astype(jnp.float32)
    return lanes_dot(hot, coef)


def halves(value, block):
    return jnp.concatenate([value[:, 0:block], value[:, block : 2 * block]], axis=0)


def factor_kernel(tile_count, knot_count, block, index, shared, factors, chosen, coef, local, system):
    total = tile_count * knot_count
    bands = jnp.sum(shared[...].reshape(tile_count, knot_count, SUB, LANES), axis=1)
    labels = shared[...].reshape(tile_count, knot_count, SUB, LANES)[:, 0, BAND, :]
    labels = jnp.concatenate([labels[:, 0:1], labels[:, 1:2]], axis=0)
    lane = lax.broadcasted_iota(jnp.int32, (2 * tile_count, LANES), 1).astype(jnp.float32)
    select = (lane == labels).astype(jnp.float32)
    chosen[...] = select
    row = lax.broadcasted_iota(jnp.int32, (total, LANES), 0)
    col = lax.broadcasted_iota(jnp.int32, (total, LANES), 1)
    start = cols_dot(shared[:, BAND + 1, 0:block], (row == col).astype(jnp.float32))
    coef[...] = start
    local[...] = local_rows(index, start)
    for d in range(BAND):
        system[d] = cols_dot(halves(bands[:, d, :], block), select)
    penalty = smoothing(block)

    def entry(k, d):
        extra = smooth_weight * float(penalty[k - d, k]) + (ridge_weight if d == 0 else 0.0)
        return jnp.broadcast_to(system[d, k - d : k - d + 1, :], (SUB, LANES)) + extra

    zero = jnp.zeros((SUB, LANES), jnp.float32)
    rows = []
    for k in range(block):
        p1, q1, r1, i1 = rows[k - 1] if k >= 1 else (zero,) * 4
        p2, q2, r2, i2 = rows[k - 2] if k >= 2 else (zero,) * 4
        p3, q3, r3, i3 = rows[k - 3] if k >= 3 else (zero,) * 4
        ur = entry(k, 3) if k >= 3 else zero
        uq = entry(k, 2) - ur * p2 if k >= 2 else zero
        up = entry(k, 1) - ur * q1 - uq * p1 if k >= 1 else zero
        r, q, p = ur * i3, uq * i2, up * i1
        inverse = 1.0 / (entry(k, 0) - ur * r - uq * q - up * p)
        rows.append((p, q, r, inverse))
        for which, value in enumerate((p, q, r, inverse)):
            factors[which, k] = value


def solve_kernel(
    tile_count, knot_count, block, index, shared, chosen, factors, coef, penalty,
    coef_out, local, work,
):
    sums = jnp.sum(shared[...].reshape(tile_count, knot_count, SUB, LANES), axis=1)
    own, lower, upper = sums[:, 0, :], sums[:, 1, :], sums[:, 2, :]
    none = jnp.zeros((1, LANES), jnp.float32)
    grads = (
        own
        + jnp.concatenate([lower[1:, :], none], axis=0)
        + jnp.concatenate([none, upper[:-1, :]], axis=0)
    )
    grad_sum = cols_dot(halves(grads, block), chosen[...])
    bend = jnp.dot(
        penalty[...], coef[...], precision=HIGHEST, preferred_element_type=jnp.float32
    )
    work[...] = -(grad_sum + smooth_weight * bend)
    forward = []
    for k in range(block):
        value = jnp.broadcast_to(work[k : k + 1, :], (SUB, LANES))
        for back in (3, 2, 1):
            if k >= back:
                value = value - factors[back - 1, k] * forward[k - back]
        forward.append(value)
    steps = [None] * block
    for k in reversed(range(block)):
        value = forward[k] * factors[3, k]
        for ahead in (3, 2, 1):
            if k + ahead < block:
                value = value - factors[ahead - 1, k + ahead] * steps[k + ahead]
        steps[k] = value
        work[k : k + 1, :] = value[0:1, :]
    fresh = coef[...] + work[...]
    coef_out[...] = fresh
    local[...] = local_rows(index, fresh)


def warp_kernel(plane, knots, depth, coef, rigid, basis, image, slope, out):
    step = pl.program_id(0)
    base = shift_step * rigid[0].astype(jnp.float32)
    count = basis.shape[0] // WINDOW

    def body(at, _):
        group = step * count + at
        first = first_knot(group, plane, knots)
        value = jnp.zeros((SUB, LANES), jnp.float32)
        for i in range(WINDOW):
            value += coef[first + i] * basis[at * WINDOW + i]
        value += base
        for r in range(SUB):
            here = pl.ds(pl.multiple_of((at * SUB + r) * depth, depth), depth)
            out[here, :] = image[here, :] + slope[here, :] * value[r : r + 1, :]
        return 0

    lax.fori_loop(0, count, body, 0)


def per_device(images, gradient, shifts, tile_blocks, intersections, start_coefficients):
    depth, plane = images.shape[1:]
    block = start_coefficients.shape[1]
    knots = 2 * block
    groups = plane // GROUP
    rows = plane // LANES
    padded = FRONT + rows + BACK
    tile_count = lax.axis_size("tile")
    knot_count = lax.axis_size("knot")
    total = tile_count * knot_count
    cap = intersections.shape[2]
    me = lax.axis_index("tile") * knot_count + lax.axis_index("knot")
    links = intersections[0]
    table = links.reshape(3 * cap, 5)

    def flat(volume):
        volume = volume.reshape(depth, rows, LANES).transpose(1, 0, 2)
        return volume.reshape(rows * depth, LANES)

    def route(value, distance):
        pairs = [
            (i - distance, i) for i in range(tile_count) if 0 <= i - distance < tile_count
        ]
        return lax.ppermute(value, "tile", pairs)

    image, slope = flat(images[0]), flat(gradient[0])
    incoming = jnp.concatenate([route(links[2], 1), links[1], route(links[0], -1)], axis=0)
    slope_below, slope_above = flat(route(gradient, 1)[0]), flat(route(gradient, -1)[0])

    basis, weight, pull, bands, image_planes, slope_planes = pl.pallas_call(
        functools.partial(own_kernel, depth, plane, knots),
        out_shape=(
            f32(groups * WINDOW, SUB, LANES),
            f32(rows, LANES),
            f32(rows, LANES),
            f32(SUB, LANES),
            f32(depth, padded, LANES),
            f32(depth, padded, LANES),
        ),
        in_specs=[SMEM, VMEM, VMEM],
        out_specs=(VMEM,) * 6,
        scratch_shapes=[
            pltpu.VMEM((padded, LANES), jnp.float32),
            pltpu.VMEM((BAND, knots + 8, SUB, LANES), jnp.float32),
        ],
        compiler_params=PARAMS,
        cost_estimate=pl.CostEstimate(
            flops=100 * plane, bytes_accessed=12 * depth * plane, transcendentals=0
        ),
        name="own",
    )(incoming, image, slope)

    def share(value):
        return pl.pallas_call(
            functools.partial(share_kernel, knot_count, total),
            out_shape=f32(total, SUB, LANES),
            in_specs=[VMEM],
            out_specs=VMEM,
            scratch_shapes=[
                pltpu.VMEM((total, SUB, LANES), jnp.float32),
                pltpu.SemaphoreType.DMA((total,)),
                pltpu.SemaphoreType.DMA((total,)),
            ],
            compiler_params=pltpu.CompilerParams(collective_id=0, has_side_effects=True),
            name="share",
        )(value)

    def pairs(which, far):
        return pl.pallas_call(
            functools.partial(pair_kernel, depth, plane),
            out_shape=(f32(cap, SPAN * SUB, LANES),) * 2,
            in_specs=[SMEM] + [VMEM] * 3,
            out_specs=(VMEM,) * 2,
            scratch_shapes=[pltpu.VMEM((depth, padded, LANES), jnp.float32)],
            compiler_params=PARAMS,
            cost_estimate=pl.CostEstimate(
                flops=4 * depth * cap * SLAB,
                bytes_accessed=12 * depth * plane,
                transcendentals=0,
            ),
            name="pairs",
        )(links[which], far, image_planes, slope_planes)

    facts = jnp.concatenate(
        [
            bands[0:BAND],
            jnp.pad(tile_blocks.astype(jnp.float32), ((0, 0), (0, LANES - 2))),
            jnp.pad(start_coefficients, ((0, 0), (0, LANES - block))),
            bands[BAND + 2 :],
        ],
        axis=0,
    )
    index = jnp.concatenate([tile_blocks[0], me[None].astype(jnp.int32)])
    factors, chosen, coef, local = pl.pallas_call(
        functools.partial(factor_kernel, tile_count, knot_count, block),
        out_shape=(
            f32(4, block, SUB, LANES),
            f32(2 * tile_count, LANES),
            f32(block, LANES),
            f32(SUB, block),
        ),
        in_specs=[SMEM, VMEM],
        out_specs=(VMEM,) * 4,
        scratch_shapes=[pltpu.VMEM((BAND, block, LANES), jnp.float32)],
        compiler_params=PARAMS,
        name="factor",
    )(index, share(facts))
    sums = pairs(1, slope)
    sums = (*pairs(0, slope_below), *sums, *pairs(2, slope_above))
    penalty = jnp.asarray(smoothing(block))

    def scalars(rows_of):
        return jnp.pad(rows_of[0:2].reshape(knots), (0, 8))

    for step in range(ITERS):
        grads = pl.pallas_call(
            functools.partial(project_kernel, plane, knots, cap),
            out_shape=f32(SUB, LANES),
            in_specs=[SMEM] * 3 + [VMEM] * 9,
            out_specs=VMEM,
            scratch_shapes=[
                pltpu.VMEM((padded, LANES), jnp.float32),
                pltpu.VMEM((3, padded, LANES), jnp.float32),
                pltpu.VMEM((3, knots + 8, SUB, LANES), jnp.float32),
            ],
            compiler_params=PARAMS,
            name="project",
        )(table, scalars(local), shifts, basis, weight, pull, *sums)
        coef, local = pl.pallas_call(
            functools.partial(solve_kernel, tile_count, knot_count, block),
            out_shape=(f32(block, LANES), f32(SUB, block)),
            in_specs=[SMEM] + [VMEM] * 5,
            out_specs=(VMEM,) * 2,
            scratch_shapes=[pltpu.VMEM((block, LANES), jnp.float32)],
            compiler_params=PARAMS,
            name="solve",
        )(index, share(grads), chosen, factors, coef, penalty)

    cuts = 8
    part = pl.BlockSpec((rows * depth // cuts, LANES), lambda i: (i, 0))
    warped = pl.pallas_call(
        functools.partial(warp_kernel, plane, knots, depth),
        out_shape=f32(rows * depth, LANES),
        grid=(cuts,),
        in_specs=[
            SMEM,
            SMEM,
            pl.BlockSpec((groups * WINDOW // cuts, SUB, LANES), lambda i: (i, 0, 0)),
            part,
            part,
        ],
        out_specs=part,
        compiler_params=PARAMS,
        name="warp",
    )(scalars(local), shifts, basis, image, slope)
    warped = warped.reshape(rows, depth, LANES).transpose(1, 0, 2).reshape(1, depth, plane)
    return local[2:3], warped


def solution(mesh):
    placed = (
        P("tile", "knot", None),
        P("tile", "knot", None),
        P("tile"),
        P("tile", None),
        P("tile", None, None, None),
        P(("tile", "knot"), None),
    )
    return jax.shard_map(
        per_device,
        mesh=mesh,
        in_specs=placed,
        out_specs=(P(("tile", "knot"), None), P("tile", "knot", None)),
        check_vma=False,
    )
```

time: 1190 us -> 156 us (0.13); the launches traced: 1170 us -> 155 us
  local copies, waits for them, and re-layouts: 532 us -> 24.5 us
  matrix products: 453 us -> 0 us
  Pallas kernels: 0 us -> 117 us
  other arithmetic: 72.7 us -> 1.99 us
  blocking collectives: 48.8 us -> 0 us
  starting transfers between devices: 44.3 us -> 10.1 us
  between operations: 15.7 us -> 1.61 us
    gather x432 -> x0, local copies, waits for them, and re-layouts: 497 us -> none
    dot_general x15 -> x0, matrix products: 451 us -> none  [the longest x2 244 us: per_device(): jnp.einsum('pnks,ps->pnk', piece, project, precision=lax.Precision.HIGHEST)]
    pallas_call x0 -> x13, Pallas kernels: none -> 117 us  [the longest x3 72.5 us: share(): pl.pallas_call(functools.partial(share_kernel, knot_count, total), out_sh...]
    ppermute x18 -> x4, starting transfers between devices: 44.2 us -> 10.1 us  [route(): return lax.ppermute(value, 'tile', pairs)]
    all_gather x3 -> x0, blocking collectives: 31.7 us -> none  [fetch(): column = lax.all_gather(owned, 'knot', axis=0, tiled=True)]
    another operation x8 -> x0, other arithmetic: 22.8 us -> none  [the longest x2 10.7 us: per_device(): arrived = jnp.stack([below[0], slabs[1], above[0]])]
    reduce_sum x2 -> x0, other arithmetic: 22.4 us -> none  [per_device(): project = jnp.sum(slope * misfit, axis=1)]
    select_n x2 -> x0, other arithmetic: 19.4 us -> none  [the longest x1 19.4 us: spline_basis(): return jnp.where(dist < 1.0, inner, jnp.where(dist < 2.0, outer, 0.0))]
  transfers between devices with their start and end apart: 19 -> 4, of which waited for: 3 -> 0; matrix products, arithmetic and copies ran while one was open for 45% -> 2% of each run, Pallas kernels for 0% -> 44%
where the time goes in v1:
time: 156 us; the launch traced here: 155 us
  Pallas kernels  117 us (75%)
  local copies, waits for them, and re-layouts  24.5 us (16%)
  starting transfers between devices  10.1 us (6%)
  other arithmetic  1.99 us (1%)
  between operations  1.61 us (1%)
    pallas_call x3, Pallas kernels, share(): pl.pallas_call(functools.partial(share_kernel, knot_count, total), out_sh...  72.5 us
    unnamed x68, local copies, waits for them, and re-layouts  22.9 us
    pallas_call x2, Pallas kernels, per_device(): pl.pallas_call(functools.partial(project_kernel, plane, knots, cap), out_...  15.9 us
    pallas_call x3, Pallas kernels, pairs(): pl.pallas_call(functools.partial(pair_kernel, depth, plane), out_shape=(f...  12.1 us
    ppermute x4, starting transfers between devices, route(): return lax.ppermute(value, 'tile', pairs)  10.1 us
    pallas_call x1, Pallas kernels, per_device(): pl.pallas_call(functools.partial(own_kernel, depth, plane, knots), out_sh...  7.43 us
    pallas_call x1, Pallas kernels, per_device(): pl.pallas_call(functools.partial(warp_kernel, plane, knots, depth), out_s...  4.24 us
  transfers between devices with their start and end apart: 4, of which 0 were waited for; matrix products, arithmetic and copies ran while one was open for 2% of the time, Pallas kernels for 44%

profile of v1, /device:TPU:0, one launch (start us, length us, event | category | flops | bytes accessed | tf_op | source)
XLA Modules:
  0.0 155.0 jit_solution(9512403908762364935)
XLA Ops:
  0.6 1.3 collective-permute-start.3
  1.9 4.4 %collective-permute-start.2 = (f32[1,8,65536]{2,1,0:T(8,128)}, f32[1,8,65536]{2,1,0:T(8,128)}, u32[]{:S(2)}, u32[]{:S(2)}) collective-permute-start(f32[1,8,65536]{2,1,0:T(8,128)} %param.8), channel_id=1, source_target_pairs={{0,4},{4,8},{8,12},{12,16},{16,20},{20,24},{24,28},{1,5},{5,9},{9,... | collective-permute-start | bytes 6291464 | tf_op jit(solution)/shard_map/ppermute | solution.py:429
  7.1 3.1 %collective-permute-start = (s32[8,5]{1,0:T(8,128)S(1)}, s32[8,5]{1,0:T(8,128)S(1)}, u32[]{:S(2)}, u32[]{:S(2)}) collective-permute-start(s32[8,5]{1,0:T(8,128)S(1)} %get-tuple-element.40.table), channel_id=1, source_target_pairs={{0,4},{4,8},{8,12},{12,16},{16,20},{20,24},{24,28},{1,5},{5,9},{9,... | collective-permute-start | bytes 488 | tf_op jit(solution)/shard_map/ppermute | solution.py:429
  10.2 1.3 collective-permute-start.1
  13.6 1.6 %copy-done.7 = f32[1,8,65536]{2,1,0:T(8,128)S(1)} copy-done((f32[1,8,65536]{2,1,0:T(8,128)S(1)}, f32[1,8,65536]{2,1,0:T(8,128)}, u32[]{:S(2)}) %copy-start.7) | copy-done | bytes 2097176
  15.2 7.4 %own.1 = (f32[384,8,128]{2,1,0:T(8,128)S(1)}, f32[512,128]{1,0:T(8,128)S(1)}, f32[512,128]{1,0:T(8,128)S(1)}, f32[8,128]{1,0:T(8,128)S(1)}, f32[8,536,128]{2,1,0:T(8,128)}, /*index=5*/f32[8,536,128]{2,1,0:T(8,128)}) custom-call(s32[24,5]{1,0:T(8,128)S(1)} %pad_add_fusion.table, f32[4096,128]{1,0:T(8,128)S(1)} %bitcast.37, f32[4096,128]{1,0:T(8,128)} %bitcast.34), custom_call_target="tpu_custom_call" | custom-call | flops 6553600 | bytes 6291456 | tf_op jit(solution)/shard_map/own/pallas_call | solution.py:435
  22.6 1.1 copy-done.3
  25.8 50.8 %share.3.shared = f32[32,8,128]{2,1,0:T(8,128)} custom-call(f32[8,128]{1,0:T(8,128)} %fusion.mine), custom_call_target="tpu_custom_call" | custom-call | tf_op jit(solution)/shard_map/share/pallas_call | solution.py:459
  76.6 0.9 copy-done.27
  77.5 1.6 %factor.1 = (f32[4,64,8,128]{3,2,1,0:T(8,128)S(1)}, f32[16,128]{1,0:T(8,128)S(1)}, f32[64,128]{1,0:T(8,128)S(1)}, f32[8,64]{1,0:T(8,128)S(1)}) custom-call(s32[3]{0:T(128)S(1)} %pad_add_fusion.1.index, f32[32,8,128]{2,1,0:T(8,128)S(1)} %copy-done.27), custom_call_target="tpu_custom_call" | custom-call | tf_op jit(solution)/shard_map/factor/pallas_call | solution.py:499
  79.2 1.6 %copy-done = f32[8,536,128]{2,1,0:T(8,128)S(1)} copy-done((f32[8,536,128]{2,1,0:T(8,128)S(1)}, f32[8,536,128]{2,1,0:T(8,128)}, u32[]{:S(2)}) %copy-start) | copy-done | bytes 2195480
  80.8 3.6 %pairs.4 = (f32[8,72,128]{2,1,0:T(8,128)S(1)}, f32[8,72,128]{2,1,0:T(8,128)S(1)}) custom-call(s32[8,5]{1,0:T(8,128)S(1)} %get-tuple-element.42.table, f32[4096,128]{1,0:T(8,128)S(1)} %bitcast.35, f32[8,536,128]{2,1,0:T(8,128)S(1)} %copy-done, f32[8,536,128]{2,1,0:T(8,128)} %get-tuple-element.27.slope_planes), custom_call_target="tpu_custom_call" | custom-call | flops 2097152 | bytes 6291456 | tf_op jit(solution)/shard_map/pairs/pallas_call | solution.py:474
  84.4 4.2 %pairs.5 = (f32[8,72,128]{2,1,0:T(8,128)S(1)}, f32[8,72,128]{2,1,0:T(8,128)S(1)}) custom-call(s32[8,5]{1,0:T(8,128)S(1)} %get-tuple-element.40.table, f32[4096,128]{1,0:T(8,128)} %bitcast.19.far_slope, f32[8,536,128]{2,1,0:T(8,128)S(1)} %copy-done.1, f32[8,536,128]{2,1,0:T(8,128)} %get-tuple-element.27.slope_planes), custom_call_target="tpu_custom_call" | custom-call | flops 2097152 | bytes 6291456 | tf_op jit(solution)/shard_map/pairs/pallas_call | solution.py:474
  88.7 4.3 %pairs.3 = (f32[8,72,128]{2,1,0:T(8,128)S(1)}, f32[8,72,128]{2,1,0:T(8,128)S(1)}) custom-call(s32[8,5]{1,0:T(8,128)S(1)} %get-tuple-element.41.table, f32[4096,128]{1,0:T(8,128)} %bitcast.14.far_slope, f32[8,536,128]{2,1,0:T(8,128)S(1)} %copy-done.1, f32[8,536,128]{2,1,0:T(8,128)} %get-tuple-element.27.slope_planes), custom_call_target="tpu_custom_call" | custom-call | flops 2097152 | bytes 6291456 | tf_op jit(solution)/shard_map/pairs/pallas_call | solution.py:474
  93.1 7.9 %project.2.mine = f32[8,128]{1,0:T(8,128)S(1)} custom-call(s32[24,5]{1,0:T(8,128)S(1)} %bitcast.39, f32[136]{0:T(256)S(1)} %pad.20.coef, s32[1]{0:T(128)S(6)} %copy.39.rigid, f32[384,8,128]{2,1,0:T(8,128)S(1)} %copy-done.4, f32[512,128]{1,0:T(8,128)S(1)} %copy-done.20, f32[512,128]{1,0:T(8,128)S(1)} %copy-done.23, f32[8,72,128]{2,1,0:T(8,128)S(1)} %get-tuple-element.28.c0, ...), custom_call_target="tpu_custom_call" | custom-call | tf_op jit(solution)/shard_map/project/pallas_call | solution.py:521
  103.1 10.9 %share.4.shared = f32[32,8,128]{2,1,0:T(8,128)} custom-call(f32[8,128]{1,0:T(8,128)} %copy-done.32), custom_call_target="tpu_custom_call" | custom-call | tf_op jit(solution)/shard_map/share/pallas_call | solution.py:459
  114.9 1.3 solve.2
  116.9 1.4 copy-done.5
  118.3 1.0 copy-done.10
  119.3 1.0 copy-done.12
  120.2 1.0 copy-done.14
  121.2 1.0 copy-done.16
  122.2 1.0 copy-done.18
  123.1 0.9 copy-done.21
  124.1 0.9 copy-done.24
  125.0 7.9 %project.3.mine = f32[8,128]{1,0:T(8,128)S(1)} custom-call(s32[24,5]{1,0:T(8,128)S(1)} %bitcast.40, f32[136]{0:T(256)S(1)} %pad.21.coef, s32[1]{0:T(128)S(6)} %copy.39.rigid, f32[384,8,128]{2,1,0:T(8,128)S(1)} %copy-done.5, f32[512,128]{1,0:T(8,128)S(1)} %copy-done.21, f32[512,128]{1,0:T(8,128)S(1)} %copy-done.24, f32[8,72,128]{2,1,0:T(8,128)S(1)} %copy-done.16, ...), custom_call_target="tpu_custom_call" | custom-call | tf_op jit(solution)/shard_map/project/pallas_call | solution.py:521
  133.6 10.9 %share.5.shared = f32[32,8,128]{2,1,0:T(8,128)} custom-call(f32[8,128]{1,0:T(8,128)} %copy-done.31), custom_call_target="tpu_custom_call" | custom-call | tf_op jit(solution)/shard_map/share/pallas_call | solution.py:459
  144.5 0.9 copy-done.25
  145.4 1.8 %solve.3 = (f32[64,128]{1,0:T(8,128)}, f32[8,64]{1,0:T(8,128)S(1)}) custom-call(s32[3]{0:T(128)S(1)} %pad_add_fusion.1.index, f32[32,8,128]{2,1,0:T(8,128)S(1)} %copy-done.25, f32[16,128]{1,0:T(8,128)S(1)} %get-tuple-element.34.chosen, f32[4,64,8,128]{3,2,1,0:T(8,128)S(1)} %get-tuple-element.35.factors, f32[64,128]{1,0:T(8,128)S(1)} %copy-done.30, ...), custom_call_target="tpu_custom_call" | custom-call | tf_op jit(solution)/shard_map/solve/pallas_call | solution.py:534
  147.7 1.4 copy-done.6
  149.1 1.6 %copy-done.8 = f32[1,8,65536]{2,1,0:T(8,128)S(1)} copy-done((f32[1,8,65536]{2,1,0:T(8,128)S(1)}, f32[1,8,65536]{2,1,0:T(8,128)}, u32[]{:S(2)}) %copy-start.8) | copy-done | bytes 2097176
  150.7 4.2 %warp.1 = f32[4096,128]{1,0:T(8,128)} custom-call(f32[136]{0:T(256)S(1)} %pad.22.coef, s32[1]{0:T(128)S(6)} %copy.39.rigid, f32[384,8,128]{2,1,0:T(8,128)S(1)} %copy-done.6, f32[4096,128]{1,0:T(8,128)S(1)} %bitcast.38, f32[4096,128]{1,0:T(8,128)S(1)} %bitcast.36), custom_call_target="tpu_custom_call" | custom-call | tf_op jit(solution)/shard_map/warp/pallas_call | solution.py:546
  (75 shorter events, 9.3 us)
Async XLA Ops:
  0.6 83.8 %collective-permute-start.3 = (f32[1,8,65536]{2,1,0:T(8,128)}, f32[1,8,65536]{2,1,0:T(8,128)}, u32[]{:S(2)}, u32[]{:S(2)}) collective-permute-start(f32[1,8,65536]{2,1,0:T(8,128)} %param.8), channel_id=1, source_target_pairs={{4,0},{8,4},{12,8},{16,12},{20,16},{24,20},{28,24},{5,1},{9,5},{13... | collective-permute-start | bytes 6291464 | tf_op jit(solution)/shard_map/ppermute | solution.py:429
  1.9 86.7 %collective-permute-start.2 = (f32[1,8,65536]{2,1,0:T(8,128)}, f32[1,8,65536]{2,1,0:T(8,128)}, u32[]{:S(2)}, u32[]{:S(2)}) collective-permute-start(f32[1,8,65536]{2,1,0:T(8,128)} %param.8), channel_id=1, source_target_pairs={{0,4},{4,8},{8,12},{12,16},{16,20},{20,24},{24,28},{1,5},{5,9},{9,... | collective-permute-start | bytes 6291464 | tf_op jit(solution)/shard_map/ppermute | solution.py:429
  7.1 6.5 %collective-permute-start = (s32[8,5]{1,0:T(8,128)S(1)}, s32[8,5]{1,0:T(8,128)S(1)}, u32[]{:S(2)}, u32[]{:S(2)}) collective-permute-start(s32[8,5]{1,0:T(8,128)S(1)} %get-tuple-element.40.table), channel_id=1, source_target_pairs={{0,4},{4,8},{8,12},{12,16},{16,20},{20,24},{24,28},{1,5},{5,9},{9,... | collective-permute-start | bytes 488 | tf_op jit(solution)/shard_map/ppermute | solution.py:429
  10.2 3.4 %collective-permute-start.1 = (s32[8,5]{1,0:T(8,128)S(1)}, s32[8,5]{1,0:T(8,128)S(1)}, u32[]{:S(2)}, u32[]{:S(2)}) collective-permute-start(s32[8,5]{1,0:T(8,128)S(1)} %get-tuple-element.41.table), channel_id=1, source_target_pairs={{4,0},{8,4},{12,8},{16,12},{20,16},{24,20},{28,24},{5,1},{9,5},{13... | collective-permute-start | bytes 488 | tf_op jit(solution)/shard_map/ppermute | solution.py:429
  13.6 1.6 %copy-start.7 = (f32[1,8,65536]{2,1,0:T(8,128)S(1)}, f32[1,8,65536]{2,1,0:T(8,128)}, u32[]{:S(2)}) copy-start(f32[1,8,65536]{2,1,0:T(8,128)} %param.7) | copy-start | bytes 6291460
  15.2 10.0 %copy-start.33 = (f32[1,64]{1,0:T(1,128)S(1)}, f32[1,64]{1,0:T(1,128)}, u32[]{:S(2)}) copy-start(f32[1,64]{1,0:T(1,128)} %param.12) | copy-start | bytes 772
  15.2 64.0 %copy-start.2 = (f32[1,8,65536]{2,1,0:T(8,128)S(1)}, f32[1,8,65536]{2,1,0:T(8,128)}, u32[]{:S(2)}) copy-start(f32[1,8,65536]{2,1,0:T(8,128)} %param.8) | copy-start | bytes 6291460
  22.6 1.1 copy-start.3
  76.5 0.9 copy-start.27
  79.2 1.6 %copy-start = (f32[8,536,128]{2,1,0:T(8,128)S(1)}, f32[8,536,128]{2,1,0:T(8,128)}, u32[]{:S(2)}) copy-start(f32[8,536,128]{2,1,0:T(8,128)} %get-tuple-element.26.image_planes) | copy-start | bytes 6586372
  80.8 3.6 %copy-start.1 = (f32[8,536,128]{2,1,0:T(8,128)S(1)}, f32[8,536,128]{2,1,0:T(8,128)}, u32[]{:S(2)}) copy-start(f32[8,536,128]{2,1,0:T(8,128)} %get-tuple-element.26.image_planes) | copy-start | bytes 6586372
  84.4 8.6 %copy-start.9 = (f32[8,72,128]{2,1,0:T(8,128)}, f32[8,72,128]{2,1,0:T(8,128)S(1)}, u32[]{:S(2)}) copy-start(f32[8,72,128]{2,1,0:T(8,128)S(1)} %get-tuple-element.31.d1) | copy-start | bytes 884740
  88.6 4.4 %copy-start.11 = (f32[8,72,128]{2,1,0:T(8,128)}, f32[8,72,128]{2,1,0:T(8,128)S(1)}, u32[]{:S(2)}) copy-start(f32[8,72,128]{2,1,0:T(8,128)S(1)} %get-tuple-element.32.c2) | copy-start | bytes 884740
  88.6 4.4 %copy-start.13 = (f32[8,72,128]{2,1,0:T(8,128)}, f32[8,72,128]{2,1,0:T(8,128)S(1)}, u32[]{:S(2)}) copy-start(f32[8,72,128]{2,1,0:T(8,128)S(1)} %get-tuple-element.33.d2) | copy-start | bytes 884740
  88.6 4.4 %copy-start.4 = (f32[384,8,128]{2,1,0:T(8,128)S(1)}, f32[384,8,128]{2,1,0:T(8,128)}, u32[]{:S(2)}) copy-start(f32[384,8,128]{2,1,0:T(8,128)} %copy-done.3) | copy-start | bytes 4718596
  88.7 4.4 %copy-start.20 = (f32[512,128]{1,0:T(8,128)S(1)}, f32[512,128]{1,0:T(8,128)}, u32[]{:S(2)}) copy-start(f32[512,128]{1,0:T(8,128)} %copy-done.19) | copy-start | bytes 786436
  88.7 4.4 %copy-start.23 = (f32[512,128]{1,0:T(8,128)S(1)}, f32[512,128]{1,0:T(8,128)}, u32[]{:S(2)}) copy-start(f32[512,128]{1,0:T(8,128)} %copy-done.22) | copy-start | bytes 786436
  93.0 21.0 %copy-start.28 = (f32[64,64]{1,0:T(8,128)S(1)}, f32[64,64]{1,0:T(8,128)}, u32[]{:S(2)}) copy-start(f32[64,64]{1,0:T(8,128)} %constant.16.clone.penalty) | copy-start | bytes 49156
  101.7 0.7 copy-start.17
  114.0 0.9 copy-start.26
  116.9 1.4 copy-start.5
  118.3 1.0 copy-start.10
  119.3 1.0 copy-start.12
  120.2 1.0 copy-start.14
  121.2 1.0 copy-start.16
  122.2 1.0 copy-start.18
  123.1 0.9 copy-start.21
  124.1 0.9 copy-start.24
  125.0 19.4 %copy-start.30 = (f32[64,128]{1,0:T(8,128)S(1)}, f32[64,128]{1,0:T(8,128)}, u32[]{:S(2)}) copy-start(f32[64,128]{1,0:T(8,128)} %copy-done.29) | copy-start | bytes 98308
  144.5 0.9 copy-start.25
  147.7 1.4 copy-start.6
  149.1 1.6 %copy-start.8 = (f32[1,8,65536]{2,1,0:T(8,128)S(1)}, f32[1,8,65536]{2,1,0:T(8,128)}, u32[]{:S(2)}) copy-start(f32[1,8,65536]{2,1,0:T(8,128)} %param.7) | copy-start | bytes 6291460
  (6 other events, 4.0 us)

commit v2 on v0

v2 whole, which is shorter than its diff:
```python
import functools
import math

import jax
import jax.numpy as jnp
import numpy as np
from jax import lax
from jax.experimental import pallas as pl
from jax.experimental.pallas import tpu as pltpu
from jax.sharding import PartitionSpec as P

SLAB = 8192
ITERS = 2
LANES = 128
SUB = 8
GROUP = SUB * LANES
FRONT = 8
BACK = 16
WINDOW = 6
BAND = 4
CHUNKS = 4
SPAN = SLAB // GROUP + 1

shift_step = 0.05
smooth_weight = 20.0
ridge_weight = 1.0
HIGHEST = lax.Precision.HIGHEST
MESH = pl.DeviceIdType.MESH
VMEM = pl.BlockSpec(memory_space=pltpu.VMEM)
SMEM = pl.BlockSpec(memory_space=pltpu.SMEM)
ANY = pl.BlockSpec(memory_space=pl.ANY)
PARAMS = pltpu.CompilerParams(vmem_limit_bytes=16 * 1024 * 1024)


def f32(*shape):
    return jax.ShapeDtypeStruct(shape, jnp.float32)


def smoothing(block):
    second = np.zeros((block - 2, block), np.float32)
    for row in range(block - 2):
        second[row, row : row + 3] = (1.0, -2.0, 1.0)
    return second.T @ second


def cols_dot(left, right):
    return lax.dot_general(
        left, right, (((0,), (0,)), ((), ())), precision=HIGHEST,
        preferred_element_type=jnp.float32,
    )


def lanes_dot(left, right):
    return lax.dot_general(
        left, right, (((1,), (1,)), ((), ())), precision=HIGHEST,
        preferred_element_type=jnp.float32,
    )


def grid_iota():
    sub = lax.broadcasted_iota(jnp.int32, (SUB, LANES), 0)
    lane = lax.broadcasted_iota(jnp.int32, (SUB, LANES), 1)
    return sub, lane


def first_knot(group, plane, knots):
    return lax.div(group * (GROUP * (knots - 3)), plane)


def clear(ref):
    ref[...] = jnp.zeros(ref.shape, ref.dtype)


def lane_sums(partial):
    return lanes_dot(jnp.ones((SUB, LANES), jnp.float32), jnp.sum(partial, axis=1))[0:1, :]


def row_sums(values):
    sub = lax.broadcasted_iota(jnp.int32, (SUB, LANES), 0)
    for bit in (1, 2, 4):
        low = (sub & bit) == 0
        values = [
            jnp.where(low, a, b) + pltpu.roll(jnp.where(low, b, a), bit, 0)
            for a, b in zip(values[0::2], values[1::2])
        ]
    return values[0]


def spread(ref, row):
    return jnp.broadcast_to(ref[row : row + 1, :], (SUB, LANES))


def greet(tile_count, knot_count):
    tile, knot = lax.axis_index("tile"), lax.axis_index("knot")
    barrier = pltpu.get_barrier_semaphore()
    for step in range(1, knot_count):
        pl.semaphore_signal(
            barrier, inc=1, device_id=(tile, lax.rem(knot + step, knot_count)), device_id_type=MESH
        )

    def call(step, _):
        pl.semaphore_signal(
            barrier, inc=1, device_id=(lax.rem(tile + step, tile_count), knot), device_id_type=MESH
        )
        return 0

    lax.fori_loop(1, tile_count, call, 0)
    pl.semaphore_wait(barrier, tile_count + knot_count - 2)


def share_scratch(tile_count, knot_count, rows):
    return [
        pltpu.VMEM((rows, LANES), jnp.float32),
        pltpu.VMEM((knot_count, rows, LANES), jnp.float32),
        pltpu.VMEM((tile_count, rows, LANES), jnp.float32),
        pltpu.SemaphoreType.DMA((knot_count,)),
        pltpu.SemaphoreType.DMA((knot_count,)),
        pltpu.SemaphoreType.DMA((tile_count,)),
        pltpu.SemaphoreType.DMA((tile_count,)),
    ]


def share(tile_count, knot_count, mine, scratch, between=None):
    total, column, table, send_a, recv_a, send_b, recv_b = scratch
    tile, knot = lax.axis_index("tile"), lax.axis_index("knot")

    def over_knot(step, slot):
        return pltpu.make_async_remote_copy(
            src_ref=mine,
            dst_ref=column.at[slot],
            send_sem=send_a.at[step],
            recv_sem=recv_a.at[slot],
            device_id=(tile, lax.rem(knot + step, knot_count)),
            device_id_type=MESH,
        )

    def over_tile(step, slot):
        return pltpu.make_async_remote_copy(
            src_ref=total,
            dst_ref=table.at[slot],
            send_sem=send_b.at[step],
            recv_sem=recv_b.at[slot],
            device_id=(lax.rem(tile + step, tile_count), knot),
            device_id_type=MESH,
        )

    for step in range(1, knot_count):
        over_knot(step, knot).start()
    column[knot] = mine[...]
    if between is not None:
        between(0)
    for step in range(1, knot_count):
        over_knot(step, lax.rem(knot + step, knot_count)).wait_recv()
    total[...] = jnp.sum(column[...], axis=0)

    def send(step, _):
        over_tile(step, tile).start()
        return 0

    lax.fori_loop(1, tile_count, send, 0)
    table[tile] = total[...]
    if between is not None:
        between(1)

    def arrive(step, _):
        over_tile(step, lax.rem(tile + step, tile_count)).wait_recv()
        return 0

    lax.fori_loop(1, tile_count, arrive, 0)

    def finish():
        for step in range(1, knot_count):
            over_knot(step, knot).wait_send()

        def sent(step, _):
            over_tile(step, tile).wait_send()
            return 0

        lax.fori_loop(1, tile_count, sent, 0)

    return table, finish


def halves(value, block):
    return jnp.concatenate([value[:, 0:block], value[:, block : 2 * block]], axis=0)


def spread_coef(blocks, coef, out):
    block = coef.shape[0]
    sub = lax.broadcasted_iota(jnp.int32, (LANES, LANES), 0)
    for n in range(2):
        hot = (sub == blocks[0, n]).astype(jnp.float32)
        out[n * block : (n + 1) * block, :] = jnp.dot(
            coef, hot, precision=HIGHEST, preferred_element_type=jnp.float32
        )
    out[2 * block : 2 * block + SUB, :] = jnp.zeros((SUB, LANES), jnp.float32)


def factor(block, penalty, system, factors):
    def entry(k, d):
        extra = smooth_weight * float(penalty[k - d, k]) + (ridge_weight if d == 0 else 0.0)
        return spread(system.at[d], k - d) + extra

    zero = jnp.zeros((SUB, LANES), jnp.float32)
    rows = []
    for k in range(block):
        p1, q1, r1, i1 = rows[k - 1] if k >= 1 else (zero,) * 4
        p2, q2, r2, i2 = rows[k - 2] if k >= 2 else (zero,) * 4
        p3, q3, r3, i3 = rows[k - 3] if k >= 3 else (zero,) * 4
        ur = entry(k, 3) if k >= 3 else zero
        uq = entry(k, 2) - ur * p2 if k >= 2 else zero
        up = entry(k, 1) - ur * q1 - uq * p1 if k >= 1 else zero
        r, q, p = ur * i3, uq * i2, up * i1
        inverse = 1.0 / (entry(k, 0) - ur * r - uq * q - up * p)
        rows.append((p, q, r, inverse))
        for which, value in enumerate((p, q, r, inverse)):
            factors[which, k] = value


def pair_place(table, side, pair):
    low = table[0, side, pair, 1] & (GROUP - 1)
    start = table[0, side, pair, 1] - low
    shift = table[0, side, pair, 3] - low
    row_b = pl.multiple_of(FRONT + lax.shift_right_logical(start, 7), SUB)
    row_a = FRONT + lax.shift_right_arithmetic(shift, 7)
    return low, row_b, row_a, shift & (LANES - 1)


def pair_sums(table, side, cap, far, image, slope, image_sum, slope_sum):
    sub, lane = grid_iota()
    place0 = sub * LANES + lane

    def body(at, _):
        pair = side * cap + at
        low, row_b, row_a, turn = pair_place(table, side, at)
        live = table[0, side, at, 4].astype(jnp.float32)
        back = (LANES - turn) & (LANES - 1)
        keep = lane >= turn
        for i in range(SPAN):
            c, d = [], []
            for r in range(SUB):
                row = i * SUB + r
                a = jnp.where(keep, far[row_a + row], far[row_a + (row + 1)])
                a = pltpu.roll(a, back, 1)
                c.append(a * image[row_b + row])
                d.append(a * slope[row_b + row])
            s = place0 + (i * GROUP - low)
            inside = (s >= 0) & (s < SLAB) & (live != 0.0)
            image_sum[pair, pl.ds(i * SUB, SUB), :] = jnp.where(inside, row_sums(c) * live, 0.0)
            slope_sum[pair, pl.ds(i * SUB, SUB), :] = jnp.where(inside, row_sums(d) * live, 0.0)
        return 0

    lax.fori_loop(0, cap, body, 0)


def pair_kernel(
    rows, cap, table, image, slope, below, above, image_sum, slope_sum,
    own_image, own_slope, own_below, own_above, sem,
):
    middle = pl.ds(FRONT, rows)
    loads = [
        pltpu.make_async_copy(src, dst.at[middle], sem.at[i])
        for i, (src, dst) in enumerate(
            ((image, own_image), (slope, own_slope), (below, own_below), (above, own_above))
        )
    ]
    for load in loads:
        load.start()
    loads[0].wait()
    loads[1].wait()
    pair_sums(table, 1, cap, own_slope, own_image, own_slope, image_sum, slope_sum)
    loads[2].wait()
    pair_sums(table, 0, cap, own_below, own_image, own_slope, image_sum, slope_sum)
    loads[3].wait()
    pair_sums(table, 2, cap, own_above, own_image, own_slope, image_sum, slope_sum)


def begin_kernel(
    depth, plane, block, tile_count, knot_count, cap, wide,
    blocks, table, first_coef, image, slope,
    basis, weight, pull, below, above, factors, chosen, coef, local,
    own_image, own_slope, passing, tabs, tabs_in, acc, system, mine,
    here_sem, tab_send, tab_recv, big_send, big_recv, chunk_send, chunk_recv, pass_send, pass_recv,
    *share_refs,
):
    knots = 2 * block
    rows = plane // LANES
    groups = plane // GROUP
    half, piece = rows // 2, rows // 2 // CHUNKS
    tile, knot = lax.axis_index("tile"), lax.axis_index("knot")
    pos = lax.rem(tile, wide) if wide else tile
    sub, lane = grid_iota()
    place0 = sub * LANES + lane
    land = (below, above)
    loads = [
        pltpu.make_async_copy(image, own_image, here_sem.at[0]),
        pltpu.make_async_copy(slope, own_slope, here_sem.at[1]),
    ]
    for load in loads:
        load.start()
    for d in range(3):
        for m in range(cap):
            for row, part in ((m, 3), (cap + m, 4)):
                value = table[0, d, m, part].astype(jnp.float32)
                tabs[d, row : row + 1, :] = jnp.full((1, LANES), value)
    greet(tile_count, knot_count)

    def remote(src, dst, send_sem, recv_sem, to):
        return pltpu.make_async_remote_copy(
            src_ref=src, dst_ref=dst, send_sem=send_sem, recv_sem=recv_sem,
            device_id=(to, knot), device_id_type=MESH,
        )

    def tab_copy(side):
        return remote(
            tabs.at[2 - 2 * side], tabs_in.at[side], tab_send.at[side], tab_recv.at[side],
            tile + (1 - 2 * side),
        )

    def direct(side, count):
        return remote(
            slope.at[pl.ds(0, count)], land[side].at[pl.ds(0, count)],
            big_send.at[side], big_recv.at[side], tile + (1 - 2 * side),
        )

    def to_relay(side, c):
        return remote(
            slope.at[pl.ds(half + c * piece, piece)], passing.at[pl.ds(c * piece, piece)],
            chunk_send.at[c], chunk_recv.at[c], tile + (wide - 2 * wide * side),
        )

    def from_relay(side, c):
        return remote(
            passing.at[pl.ds(c * piece, piece)],
            land[side].at[pl.ds(half + c * piece, piece)],
            pass_send.at[c], pass_recv.at[c], tile + (1 - wide if side == 0 else wide - 1),
        )

    goes = (tile + 1 < tile_count, tile > 0)
    comes = (tile > 0, tile + 1 < tile_count)
    if wide:
        edge_out = (pos == wide - 1, pos == 0)
        edge_in = (pos == 0, pos == wide - 1)
        relays = ((pos == wide - 1) & (tile >= wide), (pos == 0) & (tile + wide < tile_count))

    def when(*terms):
        flag = terms[0]
        for term in terms[1:]:
            flag = flag & term
        return pl.when(flag)

    for side in range(2):
        when(goes[side])(lambda side=side: tab_copy(side).start())
    for side in range(2):
        if wide:
            def split(side=side):
                for c in range(CHUNKS):
                    to_relay(side, c).start()
                direct(side, half).start()

            when(goes[side], edge_out[side])(split)
            when(goes[side], jnp.logical_not(edge_out[side]))(
                lambda side=side: direct(side, rows).start()
            )
        else:
            when(goes[side])(lambda side=side: direct(side, rows).start())

    def forward(c):
        if wide:
            for side in range(2):
                def hand_on(side=side):
                    to_relay(side, c).wait_recv()
                    from_relay(side, c).start()

                when(relays[side])(hand_on)

    clear(acc)
    for load in loads:
        load.wait()

    def squares(group, _):
        gg, gi = [], []
        for r in range(SUB):
            row = group * SUB + r
            g = own_slope[row]
            gg.append(g * g)
            gi.append(g * own_image[row])
        here = pl.ds(pl.multiple_of(group * SUB, SUB), SUB)
        weight[here, :] = row_sums(gg)
        pull[here, :] = row_sums(gi)
        return 0

    lax.fori_loop(0, groups, squares, 0)
    forward(0)
    for side in range(2):
        when(comes[side])(lambda side=side: tab_copy(side).wait_recv())

        def absent(side=side):
            tabs_in[side] = jnp.zeros((2 * cap, LANES), jnp.float32)

        when(jnp.logical_not(comes[side]))(absent)

    def body(group, _):
        here = pl.ds(pl.multiple_of(group * SUB, SUB), SUB)
        at = (place0 + group * GROUP).astype(jnp.float32)
        count = jnp.zeros((SUB, LANES), jnp.float32)
        for source in (tabs_in.at[0], tabs.at[1], tabs_in.at[1]):
            for m in range(cap):
                s = at - spread(source, m)
                inside = (s >= 0.0) & (s < float(SLAB))
                count += jnp.where(inside, spread(source, cap + m), 0.0)
        w = weight[here, :] * count
        weight[here, :] = w
        pull[here, :] = pull[here, :] * count
        first = first_knot(group, plane, knots)
        place = at * ((knots - 3) / plane) + 1.0
        parts = []
        for i in range(WINDOW):
            dist = jnp.abs(place - (first + i).astype(jnp.float32))
            inner = 2.0 / 3.0 - dist * dist + 0.5 * dist * dist * dist
            outer = (2.0 - dist) * (2.0 - dist) * (2.0 - dist) * (1.0 / 6.0)
            value = jnp.where(dist < 1.0, inner, jnp.where(dist < 2.0, outer, 0.0))
            basis[group * WINDOW + i] = value
            parts.append(value)
        for i in range(WINDOW):
            scaled = parts[i] * w
            for d in range(min(BAND, WINDOW - i)):
                acc[d, first + i] += scaled * parts[i + d]
        return 0

    lax.fori_loop(0, groups, body, 0)
    forward(1)
    clear(mine)
    for d in range(BAND):
        mine[d : d + 1, :] = lane_sums(acc[d, 0:knots])
    lane_row = lax.broadcasted_iota(jnp.int32, (1, LANES), 1)
    label = jnp.where(
        lane_row == 0,
        blocks[0, 0].astype(jnp.float32),
        jnp.where(lane_row == 1, blocks[0, 1].astype(jnp.float32), 0.0),
    )
    mine[BAND : BAND + 1, :] = jnp.where(knot == 0, label, 0.0)
    mine[pl.ds(SUB + knot, 1), 0:block] = first_coef[...]
    shared, finish = share(
        tile_count, knot_count, mine, share_refs, lambda stage: forward(2 + stage)
    )
    bands = shared[...]
    labels = bands[:, BAND, :]
    labels = jnp.concatenate([labels[:, 0:1], labels[:, 1:2]], axis=0)
    wide_lane = lax.broadcasted_iota(jnp.int32, (2 * tile_count, LANES), 1).astype(jnp.float32)
    select = (wide_lane == labels).astype(jnp.float32)
    chosen[...] = select
    row = lax.broadcasted_iota(jnp.int32, (tile_count, LANES), 0) * knot_count
    col = lax.broadcasted_iota(jnp.int32, (tile_count, LANES), 1)
    start = jnp.zeros((block, LANES), jnp.float32)
    for k in range(knot_count):
        start += cols_dot(bands[:, SUB + k, 0:block], (row + k == col).astype(jnp.float32))
    coef[...] = start
    spread_coef(blocks, start, local)
    for d in range(BAND):
        system[d] = cols_dot(halves(bands[:, d, :], block), select)
    factor(block, smoothing(block), system, factors)

    for side in range(2):
        if wide:
            def pieces(side=side):
                direct(side, half).wait_recv()
                for c in range(CHUNKS):
                    from_relay(side, c).wait_recv()

            when(comes[side], edge_in[side])(pieces)
            when(comes[side], jnp.logical_not(edge_in[side]))(
                lambda side=side: direct(side, rows).wait_recv()
            )
        else:
            when(comes[side])(lambda side=side: direct(side, rows).wait_recv())
    finish()
    for side in range(2):
        when(goes[side])(lambda side=side: tab_copy(side).wait_send())
        if wide:
            def sent(side=side):
                for c in range(CHUNKS):
                    to_relay(side, c).wait_send()
                direct(side, half).wait_send()

            when(goes[side], edge_out[side])(sent)
            when(goes[side], jnp.logical_not(edge_out[side]))(
                lambda side=side: direct(side, rows).wait_send()
            )

            def passed(side=side):
                for c in range(CHUNKS):
                    from_relay(side, c).wait_send()

            when(relays[side])(passed)
        else:
            when(goes[side])(lambda side=side: direct(side, rows).wait_send())


def fill_field(groups, plane, knots, base, local, basis, store):
    for group in range(groups):
        first = group * GROUP * (knots - 3) // plane
        value = spread(local, first) * basis[group * WINDOW]
        for i in range(1, WINDOW):
            value += spread(local, first + i) * basis[group * WINDOW + i]
        store(group, value + base)


def project_kernel(
    plane, knots, cap, table, rigid, local, basis, weight, pull, image_sum, slope_sum,
    grads, field, landed, moved,
):
    groups = plane // GROUP
    rows = plane // LANES
    sub, lane = grid_iota()
    field[0:FRONT, :] = jnp.zeros((FRONT, LANES), jnp.float32)
    field[FRONT + rows : FRONT + rows + BACK, :] = jnp.zeros((BACK, LANES), jnp.float32)
    clear(landed)
    clear(moved)
    base = shift_step * rigid[0].astype(jnp.float32)

    def store(group, value):
        field[FRONT + group * SUB : FRONT + (group + 1) * SUB, :] = value

    fill_field(groups, plane, knots, base, local, basis, store)

    for side in range(3):

        def body(pair, _):
            at_pair = side * cap + pair
            low, row_b, row_a, turn = pair_place(table, side, pair)
            keep = lane < LANES - turn
            slot = pair & 1
            for i in range(SPAN):
                at = pl.ds(pl.multiple_of(row_b + i * SUB, SUB), SUB)
                here = pl.ds(i * SUB, SUB)
                moved[slot, pl.ds(SUB + i * SUB, SUB), :] = (
                    image_sum[at_pair, here, :] + field[at, :] * slope_sum[at_pair, here, :]
                )
            for i in range(SPAN + 1):
                term = jnp.where(
                    keep,
                    moved[slot, pl.ds(SUB + i * SUB, SUB), :],
                    moved[slot, pl.ds(SUB + i * SUB - 1, SUB), :],
                )
                landed[side, pl.ds(row_a + i * SUB, SUB), :] += pltpu.roll(term, turn, 1)
            return 0

        lax.fori_loop(0, cap, body, 0)

    def own(group, _):
        at = pl.ds(pl.multiple_of(FRONT + group * SUB, SUB), SUB)
        here = pl.ds(pl.multiple_of(group * SUB, SUB), SUB)
        landed[1, at, :] = landed[1, at, :] - pull[here, :] - weight[here, :] * field[at, :]
        return 0

    lax.fori_loop(0, groups, own, 0, unroll=4)
    holders = [[] for _ in range(knots)]
    for group in range(groups):
        first = group * GROUP * (knots - 3) // plane
        for i in range(WINDOW):
            if first + i < knots:
                holders[first + i].append((group, group * WINDOW + i))
    for q, side in enumerate((1, 0, 2)):
        parts = []
        for j in range(knots):
            total = None
            for group, at in holders[j]:
                term = basis[at] * landed[side, FRONT + group * SUB : FRONT + (group + 1) * SUB, :]
                total = term if total is None else total + term
            parts.append(total)
        parts = [row_sums(parts[j : j + SUB]) for j in range(0, knots, SUB)]
        sums = jnp.concatenate(parts, axis=0)
        line = lanes_dot(jnp.ones((SUB, LANES), jnp.float32), sums)
        grads[q : q + 1, :] = -line[0:1, :]
    grads[3:SUB, :] = jnp.zeros((SUB - 3, LANES), jnp.float32)


def settle_kernel(
    tile_count, knot_count, block, blocks, mine, chosen, factors, coef, penalty,
    coef_out, local, own_out, work, *share_refs,
):
    greet(tile_count, knot_count)
    shared, finish = share(tile_count, knot_count, mine, share_refs)
    sums = shared[...]
    own, lower, upper = sums[:, 0, :], sums[:, 1, :], sums[:, 2, :]
    none = jnp.zeros((1, LANES), jnp.float32)
    grads = (
        own
        + jnp.concatenate([lower[1:, :], none], axis=0)
        + jnp.concatenate([none, upper[:-1, :]], axis=0)
    )
    grad_sum = cols_dot(halves(grads, block), chosen[...])
    bend = jnp.dot(
        penalty[...], coef[...], precision=HIGHEST, preferred_element_type=jnp.float32
    )
    work[...] = -(grad_sum + smooth_weight * bend)
    forward = []
    for k in range(block):
        value = spread(work, k)
        for back in (3, 2, 1):
            if k >= back:
                value = value - factors[back - 1, k] * forward[k - back]
        forward.append(value)
    steps = [None] * block
    for k in reversed(range(block)):
        value = forward[k] * factors[3, k]
        for ahead in (3, 2, 1):
            if k + ahead < block:
                value = value - factors[ahead - 1, k + ahead] * steps[k + ahead]
        steps[k] = value
        work[k : k + 1, :] = value[0:1, :]
    fresh = coef[...] + work[...]
    coef_out[...] = fresh
    spread_coef(blocks, fresh, local)
    lane = lax.broadcasted_iota(jnp.int32, (SUB, LANES), 1)
    me = lax.axis_index("tile") * knot_count + lax.axis_index("knot")
    own_out[...] = lanes_dot((lane == me).astype(jnp.float32), fresh)
    finish()


def warp_kernel(plane, knots, depth, rigid, local, basis, image, slope, out):
    step = pl.program_id(0)
    base = shift_step * rigid[0].astype(jnp.float32)
    count = basis.shape[0] // WINDOW

    def body(at, _):
        first = first_knot(step * count + at, plane, knots)
        value = jnp.zeros((SUB, LANES), jnp.float32)
        for i in range(WINDOW):
            value += jnp.broadcast_to(local[pl.ds(first + i, 1), :], (SUB, LANES)) * basis[
                at * WINDOW + i
            ]
        value += base
        for r in range(SUB):
            row = at * SUB + r
            out[row] = image[row] + slope[row] * value[r : r + 1, :]
        return 0

    lax.fori_loop(0, count, body, 0, unroll=2)


def per_device(images, gradient, shifts, tile_blocks, intersections, start_coefficients):
    depth, plane = images.shape[1:]
    block = start_coefficients.shape[1]
    knots = 2 * block
    groups = plane // GROUP
    rows = plane // LANES
    padded = FRONT + rows + BACK
    tile_count = lax.axis_size("tile")
    knot_count = lax.axis_size("knot")
    cap = intersections.shape[2]
    side = math.isqrt(tile_count // 2)
    wide = 2 * side if side > 1 and 2 * side * side == tile_count else 0

    def flat(volume):
        return volume.reshape(depth, rows, LANES).transpose(1, 0, 2)

    image, slope = flat(images[0]), flat(gradient[0])
    volume = pltpu.VMEM((padded, SUB, LANES), jnp.float32)
    pair_of = pltpu.SemaphoreType.DMA((2,))
    chunk_of = pltpu.SemaphoreType.DMA((CHUNKS,))

    basis, weight, pull, below, above, factors, chosen, coef, local = pl.pallas_call(
        functools.partial(
            begin_kernel, depth, plane, block, tile_count, knot_count, cap, wide
        ),
        out_shape=(
            f32(groups * WINDOW, SUB, LANES),
            f32(rows, LANES),
            f32(rows, LANES),
            f32(rows, SUB, LANES),
            f32(rows, SUB, LANES),
            f32(4, block, SUB, LANES),
            f32(2 * tile_count, LANES),
            f32(block, LANES),
            f32(knots + SUB, LANES),
        ),
        in_specs=[SMEM, SMEM, VMEM, ANY, ANY],
        out_specs=(VMEM,) * 3 + (ANY,) * 2 + (VMEM,) * 4,
        scratch_shapes=[
            pltpu.VMEM((rows, SUB, LANES), jnp.float32),
            pltpu.VMEM((rows, SUB, LANES), jnp.float32),
            pltpu.VMEM((rows // 2, SUB, LANES), jnp.float32),
            pltpu.VMEM((3, 2 * cap, LANES), jnp.float32),
            pltpu.VMEM((2, 2 * cap, LANES), jnp.float32),
            pltpu.VMEM((BAND, knots + SUB, SUB, LANES), jnp.float32),
            pltpu.VMEM((BAND, block, LANES), jnp.float32),
            pltpu.VMEM((2 * SUB, LANES), jnp.float32),
            pair_of, pair_of, pair_of, pair_of, pair_of,
            chunk_of, chunk_of, chunk_of, chunk_of,
            *share_scratch(tile_count, knot_count, 2 * SUB),
        ],
        compiler_params=pltpu.CompilerParams(
            collective_id=0, has_side_effects=True, vmem_limit_bytes=48 * 1024 * 1024
        ),
        name="begin",
    )(tile_blocks, intersections, start_coefficients, image, slope)
    image_sum, slope_sum = pl.pallas_call(
        functools.partial(pair_kernel, rows, cap),
        out_shape=(f32(3 * cap, SPAN * SUB, LANES),) * 2,
        in_specs=[SMEM] + [ANY] * 4,
        out_specs=(VMEM,) * 2,
        scratch_shapes=[volume] * 4 + [pltpu.SemaphoreType.DMA((4,))],
        compiler_params=pltpu.CompilerParams(vmem_limit_bytes=48 * 1024 * 1024),
        name="pairs",
    )(intersections, image, slope, below, above)
    penalty = jnp.asarray(smoothing(block))

    for step in range(ITERS):
        grads = pl.pallas_call(
            functools.partial(project_kernel, plane, knots, cap),
            out_shape=f32(SUB, LANES),
            in_specs=[SMEM] * 2 + [VMEM] * 6,
            out_specs=VMEM,
            scratch_shapes=[
                pltpu.VMEM((padded, LANES), jnp.float32),
                pltpu.VMEM((3, padded, LANES), jnp.float32),
                pltpu.VMEM((2, (SPAN + 3) * SUB, LANES), jnp.float32),
            ],
            compiler_params=PARAMS,
            name="project",
        )(intersections, shifts, local, basis, weight, pull, image_sum, slope_sum)
        coef, local, own = pl.pallas_call(
            functools.partial(settle_kernel, tile_count, knot_count, block),
            out_shape=(f32(block, LANES), f32(knots + SUB, LANES), f32(SUB, block)),
            in_specs=[SMEM] + [VMEM] * 5,
            out_specs=(VMEM,) * 3,
            scratch_shapes=[
                pltpu.VMEM((block, LANES), jnp.float32),
                *share_scratch(tile_count, knot_count, SUB),
            ],
            compiler_params=pltpu.CompilerParams(
                collective_id=1, has_side_effects=True, vmem_limit_bytes=16 * 1024 * 1024
            ),
            name="settle",
        )(tile_blocks, grads, chosen, factors, coef, penalty)

    cuts = 8
    part = pl.BlockSpec((rows // cuts, SUB, LANES), lambda i: (i, 0, 0))
    warped = pl.pallas_call(
        functools.partial(warp_kernel, plane, knots, depth),
        out_shape=f32(rows, depth, LANES),
        grid=(cuts,),
        in_specs=[
            SMEM,
            pl.BlockSpec((knots + SUB, LANES), lambda i: (0, 0)),
            pl.BlockSpec((groups * WINDOW // cuts, SUB, LANES), lambda i: (i, 0, 0)),
            part,
            part,
        ],
        out_specs=part,
        compiler_params=pltpu.CompilerParams(vmem_limit_bytes=56 * 1024 * 1024),
        name="warp",
    )(shifts, local, basis, image, slope)
    return own[0:1], warped.transpose(1, 0, 2).reshape(1, depth, plane)


def solution(mesh):
    placed = (
        P("tile", "knot", None),
        P("tile", "knot", None),
        P("tile"),
        P("tile", None),
        P("tile", None, None, None),
        P(("tile", "knot"), None),
    )
    return jax.shard_map(
        per_device,
        mesh=mesh,
        in_specs=placed,
        out_specs=(P(("tile", "knot"), None), P("tile", "knot", None)),
        check_vma=False,
    )
```

time: 1190 us -> 93.9 us (0.08); the launches traced: 1170 us -> 93.5 us
  local copies, waits for them, and re-layouts: 532 us -> 4.56 us
  matrix products: 453 us -> 0 us
  Pallas kernels: 0 us -> 87.6 us
  other arithmetic: 72.7 us -> 0 us
  blocking collectives: 48.8 us -> 0 us
  starting transfers between devices: 44.3 us -> 0 us
  between operations: 15.7 us -> 1.36 us
    gather x432 -> x0, local copies, waits for them, and re-layouts: 497 us -> none
    dot_general x15 -> x0, matrix products: 451 us -> none  [the longest x2 244 us: per_device(): jnp.einsum('pnks,ps->pnk', piece, project, precision=lax.Precision.HIGHEST)]
    pallas_call x0 -> x7, Pallas kernels: none -> 87.6 us  [the longest x1 46 us: per_device(): pl.pallas_call(functools.partial(begin_kernel, depth, plane, block, tile_...]
    ppermute x18 -> x0, starting transfers between devices: 44.2 us -> none  [the longest x12 31.3 us: from_behind(): return lax.ppermute(block, axis, route)]
    all_gather x3 -> x0, blocking collectives: 31.7 us -> none  [fetch(): column = lax.all_gather(owned, 'knot', axis=0, tiled=True)]
    another operation x8 -> x0, other arithmetic: 22.8 us -> none  [the longest x2 10.7 us: per_device(): arrived = jnp.stack([below[0], slabs[1], above[0]])]
    reduce_sum x2 -> x0, other arithmetic: 22.4 us -> none  [per_device(): project = jnp.sum(slope * misfit, axis=1)]
    select_n x2 -> x0, other arithmetic: 19.4 us -> none  [the longest x1 19.4 us: spline_basis(): return jnp.where(dist < 1.0, inner, jnp.where(dist < 2.0, outer, 0.0))]
  transfers between devices with their start and end apart: 19 -> 0, of which waited for: 3 -> 0; matrix products, arithmetic and copies ran while one was open for 45% -> 0% of each run, Pallas kernels for 0% -> 0%
where the time goes in v2:
time: 93.9 us; the launch traced here: 93.5 us
  Pallas kernels  87.6 us (93%)
  local copies, waits for them, and re-layouts  4.56 us (5%)
  between operations  1.36 us (1%)
    pallas_call x1, Pallas kernels, per_device(): pl.pallas_call(functools.partial(begin_kernel, depth, plane, block, tile_...  46 us
    pallas_call x2, Pallas kernels, per_device(): pl.pallas_call(functools.partial(settle_kernel, tile_count, knot_count, b...  21.6 us
    pallas_call x2, Pallas kernels, per_device(): pl.pallas_call(functools.partial(project_kernel, plane, knots, cap), out_...  7.9 us
    pallas_call x1, Pallas kernels, per_device(): pl.pallas_call(functools.partial(warp_kernel, plane, knots, depth), out_s...  6.66 us
    pallas_call x1, Pallas kernels, per_device(): pl.pallas_call(functools.partial(pair_kernel, rows, cap), out_shape=(f32(...  5.38 us
    unnamed x17, local copies, waits for them, and re-layouts  4.04 us

profile of v2, /device:TPU:0, one launch (start us, length us, event | category | flops | bytes accessed | tf_op | source)
XLA Modules:
  0.0 93.5 jit_solution(14630512293214304040)
XLA Ops:
  0.6 0.8 copy.12.table
  1.4 0.0 copy-start.6
  1.4 0.7 copy-done.6
  2.1 0.0 copy-start.7
  2.1 0.7 copy-done.7
  2.7 0.0 copy-start
  2.7 0.0 copy-start.1
  2.7 46.0 %begin.1 = (f32[384,8,128]{2,1,0:T(8,128)S(1)}, f32[512,128]{1,0:T(8,128)S(1)}, f32[512,128]{1,0:T(8,128)S(1)}, f32[512,8,128]{2,1,0:T(8,128)S(1)}, f32[512,8,12...) custom-call(s32[1,2]{1,0:T(1,128)S(1)} %copy-done.6, ...), custom_call_target="tpu_custom_call" | custom-call | tf_op jit(solution)/shard_map/begin/pallas_call | solution.py:664
  48.8 0.0 copy-start.3
  48.8 1.3 %copy-done.3 = f32[512,8,128]{2,1,0:T(8,128)} copy-done((f32[512,8,128]{2,1,0:T(8,128)}, f32[512,8,128]{2,1,0:T(8,128)S(1)}, u32[]{:S(2)}) %copy-start.3) | copy-done | bytes 2097176
  50.1 0.0 copy-start.2
  50.1 0.0 copy-done
  50.1 0.0 copy-done.1
  50.1 5.4 %pairs.1 = (f32[24,72,128]{2,1,0:T(8,128)S(1)}, f32[24,72,128]{2,1,0:T(8,128)S(1)}) custom-call(s32[1,3,8,5]{3,2,1,0:T(8,128)S(1)} %copy.12.table, f32[512,8,128]{2,1,0:T(8,128)S(1)} %bitcast.11, f32[512,8,128]{2,1,0:T(8,128)S(1)} %bitcast.14, f32[512,8,128]{2,1,0:T(8,128)} %copy-done.3, f32[512,8,128]{2,1,0:T(8,128)} %get-tuple-element.22.above), custom_call_target="tpu_custom_call" | custom-call | tf_op jit(solution)/shard_map/pairs/pallas_call | solution.py:699
  55.5 0.0 copy-start.4
  56.2 4.0 %project.2.mine = f32[8,128]{1,0:T(8,128)S(1)} custom-call(s32[1,3,8,5]{3,2,1,0:T(8,128)S(1)} %copy.12.table, s32[1]{0:T(128)S(6)} %copy.13.rigid, f32[136,128]{1,0:T(8,128)S(1)} %get-tuple-element.17.local, f32[384,8,128]{2,1,0:T(8,128)S(1)} %get-tuple-element.18.basis, f32[512,128]{1,0:T(8,128)S(1)} %get-tuple-element.19.weight, ...), custom_call_target="tpu_custom_call" | custom-call | tf_op jit(solution)/shard_map/project/pallas_call | solution.py:711
  60.1 0.0 copy-done.4
  60.1 10.1 %settle.2 = (f32[64,128]{1,0:T(8,128)S(1)}, f32[136,128]{1,0:T(8,128)S(1)}, f32[8,64]{1,0:T(8,128)}) custom-call(s32[1,2]{1,0:T(1,128)S(1)} %copy-done.6, f32[8,128]{1,0:T(8,128)S(1)} %project.2.mine, f32[16,128]{1,0:T(8,128)S(1)} %get-tuple-element.25.chosen, f32[4,64,8,128]{3,2,1,0:T(8,128)S(1)} %get-tuple-element.26.factors, ...), custom_call_target="tpu_custom_call" | custom-call | tf_op jit(solution)/shard_map/settle/pallas_call | solution.py:724
  70.2 0.0 copy-done.2
  70.2 3.9 %project.3.mine = f32[8,128]{1,0:T(8,128)S(1)} custom-call(s32[1,3,8,5]{3,2,1,0:T(8,128)S(1)} %copy.12.table, s32[1]{0:T(128)S(6)} %copy.13.rigid, f32[136,128]{1,0:T(8,128)S(1)} %get-tuple-element.28.local, f32[384,8,128]{2,1,0:T(8,128)S(1)} %get-tuple-element.18.basis, f32[512,128]{1,0:T(8,128)S(1)} %get-tuple-element.19.weight, ...), custom_call_target="tpu_custom_call" | custom-call | tf_op jit(solution)/shard_map/project/pallas_call | solution.py:711
  74.2 11.6 %settle.3 = (f32[64,128]{1,0:T(8,128)}, f32[136,128]{1,0:T(8,128)S(1)}, f32[8,64]{1,0:T(8,128)S(1)}) custom-call(s32[1,2]{1,0:T(1,128)S(1)} %copy-done.6, f32[8,128]{1,0:T(8,128)S(1)} %project.3.mine, f32[16,128]{1,0:T(8,128)S(1)} %get-tuple-element.25.chosen, f32[4,64,8,128]{3,2,1,0:T(8,128)S(1)} %get-tuple-element.26.factors, ...), custom_call_target="tpu_custom_call" | custom-call | tf_op jit(solution)/shard_map/settle/pallas_call | solution.py:724
  85.7 0.0 copy-start.5
  85.8 0.6 copy-done.5
  86.4 6.7 %warp.1 = f32[512,8,128]{2,1,0:T(8,128)} custom-call(s32[1]{0:T(128)S(6)} %copy.13.rigid, f32[136,128]{1,0:T(8,128)} %copy-done.5, f32[384,8,128]{2,1,0:T(8,128)} %copy-done.2, f32[512,8,128]{2,1,0:T(8,128)} %bitcast.10, f32[512,8,128]{2,1,0:T(8,128)} %bitcast.13), custom_call_target="tpu_custom_call" | custom-call | tf_op jit(solution)/shard_map/warp/pallas_call | solution.py:741
  93.0 0.5 slice.3
Async XLA Ops:
  1.4 0.7 copy-start.6
  2.1 0.7 copy-start.7
  2.7 47.4 %copy-start = (f32[1,8,65536]{2,1,0:T(8,128)S(1)}, f32[1,8,65536]{2,1,0:T(8,128)}, u32[]{:S(2)}) copy-start(f32[1,8,65536]{2,1,0:T(8,128)} %param.7) | copy-start | bytes 6291460
  2.7 47.4 %copy-start.1 = (f32[1,8,65536]{2,1,0:T(8,128)S(1)}, f32[1,8,65536]{2,1,0:T(8,128)}, u32[]{:S(2)}) copy-start(f32[1,8,65536]{2,1,0:T(8,128)} %param.8) | copy-start | bytes 6291460
  48.8 1.3 %copy-start.3 = (f32[512,8,128]{2,1,0:T(8,128)}, f32[512,8,128]{2,1,0:T(8,128)S(1)}, u32[]{:S(2)}) copy-start(f32[512,8,128]{2,1,0:T(8,128)S(1)} %get-tuple-element.21.below) | copy-start | bytes 6291460
  50.1 20.1 %copy-start.2 = (f32[384,8,128]{2,1,0:T(8,128)}, f32[384,8,128]{2,1,0:T(8,128)S(1)}, u32[]{:S(2)}) copy-start(f32[384,8,128]{2,1,0:T(8,128)S(1)} %get-tuple-element.18.basis) | copy-start | bytes 4718596
  55.5 4.6 %copy-start.4 = (f32[64,64]{1,0:T(8,128)S(1)}, f32[64,64]{1,0:T(8,128)}, u32[]{:S(2)}) copy-start(f32[64,64]{1,0:T(8,128)} %constant.2.clone.penalty) | copy-start | bytes 49156
  85.7 0.6 copy-start.5

commit v3 on v2

--- a/solution.py
+++ b/solution.py
@@ -19,6 +19,7 @@
 WINDOW = 6
 BAND = 4
 CHUNKS = 4
+CUTS = 8
 SPAN = SLAB // GROUP + 1
 
 shift_step = 0.05
@@ -90,7 +91,7 @@
     return jnp.broadcast_to(ref[row : row + 1, :], (SUB, LANES))
 
 
-def greet(tile_count, knot_count):
+def greet(tile_count, knot_count, between=None):
     tile, knot = lax.axis_index("tile"), lax.axis_index("knot")
     barrier = pltpu.get_barrier_semaphore()
     for step in range(1, knot_count):
@@ -105,6 +106,8 @@
         return 0
 
     lax.fori_loop(1, tile_count, call, 0)
+    if between is not None:
+        between()
     pl.semaphore_wait(barrier, tile_count + knot_count - 2)
 
 
@@ -148,7 +151,7 @@
         over_knot(step, knot).start()
     column[knot] = mine[...]
     if between is not None:
-        between(0)
+        between()
     for step in range(1, knot_count):
         over_knot(step, lax.rem(knot + step, knot_count)).wait_recv()
     total[...] = jnp.sum(column[...], axis=0)
@@ -159,14 +162,14 @@
 
     lax.fori_loop(1, tile_count, send, 0)
     table[tile] = total[...]
-    if between is not None:
-        between(1)
-
-    def arrive(step, _):
-        over_tile(step, lax.rem(tile + step, tile_count)).wait_recv()
-        return 0
-
-    lax.fori_loop(1, tile_count, arrive, 0)
+
+    def arrived():
+        def arrive(step, _):
+            over_tile(step, lax.rem(tile + step, tile_count)).wait_recv()
+            return 0
+
+        lax.fori_loop(1, tile_count, arrive, 0)
+        return table
 
     def finish():
         for step in range(1, knot_count):
@@ -178,7 +181,7 @@
 
         lax.fori_loop(1, tile_count, sent, 0)
 
-    return table, finish
+    return arrived, finish
 
 
 def halves(value, block):
@@ -278,9 +281,10 @@
 def begin_kernel(
     depth, plane, block, tile_count, knot_count, cap, wide,
     blocks, table, first_coef, image, slope,
-    basis, weight, pull, below, above, factors, chosen, coef, local,
-    own_image, own_slope, passing, tabs, tabs_in, acc, system, mine,
+    basis, weight, pull, below, above, bands, chosen, coef, local,
+    own_image, own_slope, passing, tabs, tabs_in, acc, mine, first, heads, columns,
     here_sem, tab_send, tab_recv, big_send, big_recv, chunk_send, chunk_recv, pass_send, pass_recv,
+    head_send, head_recv, column_send, column_recv,
     *share_refs,
 ):
     knots = 2 * block
@@ -303,7 +307,37 @@
             for row, part in ((m, 3), (cap + m, 4)):
                 value = table[0, d, m, part].astype(jnp.float32)
                 tabs[d, row : row + 1, :] = jnp.full((1, LANES), value)
+    lane_row = lax.broadcasted_iota(jnp.int32, (1, LANES), 1)
+    clear(first)
+    first[0:1, 0:block] = first_coef[...]
+    first[1:2, :] = jnp.where(
+        lane_row == 0,
+        blocks[0, 0].astype(jnp.float32),
+        jnp.where(lane_row == 1, blocks[0, 1].astype(jnp.float32), 0.0),
+    )
+    heads[tile] = first[...]
     greet(tile_count, knot_count)
+
+    def head_copy(step, slot):
+        return pltpu.make_async_remote_copy(
+            src_ref=first, dst_ref=heads.at[slot],
+            send_sem=head_send.at[step], recv_sem=head_recv.at[slot],
+            device_id=(lax.rem(tile + step, tile_count), knot), device_id_type=MESH,
+        )
+
+    def column_copy(step, slot):
+        return pltpu.make_async_remote_copy(
+            src_ref=heads, dst_ref=columns.at[slot],
+            send_sem=column_send.at[step], recv_sem=column_recv.at[slot],
+            device_id=(tile, lax.rem(knot + step, knot_count)), device_id_type=MESH,
+        )
+
+    def each(count, act):
+        def body(step, _):
+            act(step)
+            return 0
+
+        lax.fori_loop(1, count, body, 0)
 
     def remote(src, dst, send_sem, recv_sem, to):
         return pltpu.make_async_remote_copy(
@@ -351,6 +385,7 @@
 
     for side in range(2):
         when(goes[side])(lambda side=side: tab_copy(side).start())
+    each(tile_count, lambda step: head_copy(step, tile).start())
     for side in range(2):
         if wide:
             def split(side=side):
@@ -412,11 +447,11 @@
         w = weight[here, :] * count
         weight[here, :] = w
         pull[here, :] = pull[here, :] * count
-        first = first_knot(group, plane, knots)
+        knot0 = first_knot(group, plane, knots)
         place = at * ((knots - 3) / plane) + 1.0
         parts = []
         for i in range(WINDOW):
-            dist = jnp.abs(place - (first + i).astype(jnp.float32))
+            dist = jnp.abs(place - (knot0 + i).astype(jnp.float32))
             inner = 2.0 / 3.0 - dist * dist + 0.5 * dist * dist * dist
             outer = (2.0 - dist) * (2.0 - dist) * (2.0 - dist) * (1.0 / 6.0)
             value = jnp.where(dist < 1.0, inner, jnp.where(dist < 2.0, outer, 0.0))
@@ -425,41 +460,36 @@
         for i in range(WINDOW):
             scaled = parts[i] * w
             for d in range(min(BAND, WINDOW - i)):
-                acc[d, first + i] += scaled * parts[i + d]
+                acc[d, knot0 + i] += scaled * parts[i + d]
         return 0
 
-    lax.fori_loop(0, groups, body, 0)
+    lax.fori_loop(0, groups // 2, body, 0)
     forward(1)
+    lax.fori_loop(groups // 2, groups, body, 0)
+    forward(2)
     clear(mine)
     for d in range(BAND):
         mine[d : d + 1, :] = lane_sums(acc[d, 0:knots])
-    lane_row = lax.broadcasted_iota(jnp.int32, (1, LANES), 1)
-    label = jnp.where(
-        lane_row == 0,
-        blocks[0, 0].astype(jnp.float32),
-        jnp.where(lane_row == 1, blocks[0, 1].astype(jnp.float32), 0.0),
+    each(tile_count, lambda step: head_copy(step, lax.rem(tile + step, tile_count)).wait_recv())
+    each(knot_count, lambda step: column_copy(step, knot).start())
+    columns[knot] = heads[...]
+    forward(3)
+    arrived, finish = share(tile_count, knot_count, mine, share_refs)
+    each(
+        knot_count,
+        lambda step: column_copy(step, lax.rem(knot + step, knot_count)).wait_recv(),
     )
-    mine[BAND : BAND + 1, :] = jnp.where(knot == 0, label, 0.0)
-    mine[pl.ds(SUB + knot, 1), 0:block] = first_coef[...]
-    shared, finish = share(
-        tile_count, knot_count, mine, share_refs, lambda stage: forward(2 + stage)
-    )
-    bands = shared[...]
-    labels = bands[:, BAND, :]
+    labels = heads[:, 1, :]
     labels = jnp.concatenate([labels[:, 0:1], labels[:, 1:2]], axis=0)
     wide_lane = lax.broadcasted_iota(jnp.int32, (2 * tile_count, LANES), 1).astype(jnp.float32)
-    select = (wide_lane == labels).astype(jnp.float32)
-    chosen[...] = select
+    chosen[...] = (wide_lane == labels).astype(jnp.float32)
     row = lax.broadcasted_iota(jnp.int32, (tile_count, LANES), 0) * knot_count
     col = lax.broadcasted_iota(jnp.int32, (tile_count, LANES), 1)
     start = jnp.zeros((block, LANES), jnp.float32)
     for k in range(knot_count):
-        start += cols_dot(bands[:, SUB + k, 0:block], (row + k == col).astype(jnp.float32))
+        start += cols_dot(columns[k, :, 0, 0:block], (row + k == col).astype(jnp.float32))
     coef[...] = start
     spread_coef(blocks, start, local)
-    for d in range(BAND):
-        system[d] = cols_dot(halves(bands[:, d, :], block), select)
-    factor(block, smoothing(block), system, factors)
 
     for side in range(2):
         if wide:
@@ -474,7 +504,10 @@
             )
         else:
             when(comes[side])(lambda side=side: direct(side, rows).wait_recv())
+    bands[...] = arrived()[...]
     finish()
+    each(tile_count, lambda step: head_copy(step, tile).wait_send())
+    each(knot_count, lambda step: column_copy(step, knot).wait_send())
     for side in range(2):
         when(goes[side])(lambda side=side: tab_copy(side).wait_send())
         if wide:
@@ -508,7 +541,7 @@
 
 def project_kernel(
     plane, knots, cap, table, rigid, local, basis, weight, pull, image_sum, slope_sum,
-    grads, field, landed, moved,
+    landed, field, moved,
 ):
     groups = plane // GROUP
     rows = plane // LANES
@@ -555,6 +588,9 @@
         return 0
 
     lax.fori_loop(0, groups, own, 0, unroll=4)
+
+
+def project(groups, plane, knots, basis, landed, grads):
     holders = [[] for _ in range(knots)]
     for group in range(groups):
         first = group * GROUP * (knots - 3) // plane
@@ -577,12 +613,28 @@
 
 
 def settle_kernel(
-    tile_count, knot_count, block, blocks, mine, chosen, factors, coef, penalty,
-    coef_out, local, own_out, work, *share_refs,
+    tile_count, knot_count, block, plane, opening, blocks, landed, basis, chosen, given, coef,
+    penalty, coef_out, local, own_out, *refs,
 ):
-    greet(tile_count, knot_count)
-    shared, finish = share(tile_count, knot_count, mine, share_refs)
-    sums = shared[...]
+    if opening:
+        factors, work, mine, system, *share_refs = refs
+    else:
+        factors, (work, mine, *share_refs) = given, refs
+
+    def gather():
+        project(plane // GROUP, plane, 2 * block, basis, landed, mine)
+
+    def prepare():
+        if opening:
+            select = chosen[...]
+            bands = given[...]
+            for d in range(BAND):
+                system[d] = cols_dot(halves(bands[:, d, :], block), select)
+            factor(block, smoothing(block), system, factors)
+
+    greet(tile_count, knot_count, gather)
+    arrived, finish = share(tile_count, knot_count, mine, share_refs, prepare)
+    sums = arrived()[...]
     own, lower, upper = sums[:, 0, :], sums[:, 1, :], sums[:, 2, :]
     none = jnp.zeros((1, LANES), jnp.float32)
     grads = (
@@ -619,25 +671,46 @@
     finish()
 
 
-def warp_kernel(plane, knots, depth, rigid, local, basis, image, slope, out):
-    step = pl.program_id(0)
+def warp_kernel(
+    plane, knots, rigid, local, basis, image, slope, out, own_image, own_slope, field, load_sem, save_sem
+):
+    groups = plane // GROUP
+    rows = plane // LANES
+    part = rows // CUTS
     base = shift_step * rigid[0].astype(jnp.float32)
-    count = basis.shape[0] // WINDOW
-
-    def body(at, _):
-        first = first_knot(step * count + at, plane, knots)
-        value = jnp.zeros((SUB, LANES), jnp.float32)
-        for i in range(WINDOW):
-            value += jnp.broadcast_to(local[pl.ds(first + i, 1), :], (SUB, LANES)) * basis[
-                at * WINDOW + i
-            ]
-        value += base
-        for r in range(SUB):
-            row = at * SUB + r
-            out[row] = image[row] + slope[row] * value[r : r + 1, :]
-        return 0
-
-    lax.fori_loop(0, count, body, 0, unroll=2)
+
+    def load(which, cut):
+        src, dst = ((image, own_image), (slope, own_slope))[which]
+        here = pl.ds(cut * part, part)
+        return pltpu.make_async_copy(src.at[here], dst.at[here], load_sem.at[which, cut])
+
+    def save(cut):
+        here = pl.ds(cut * part, part)
+        return pltpu.make_async_copy(own_image.at[here], out.at[here], save_sem.at[cut])
+
+    for cut in range(CUTS):
+        for which in range(2):
+            load(which, cut).start()
+
+    def store(group, value):
+        field[group * SUB : (group + 1) * SUB, :] = value
+
+    fill_field(groups, plane, knots, base, local, basis, store)
+    for cut in range(CUTS):
+        for which in range(2):
+            load(which, cut).wait()
+
+        def body(group, _):
+            for r in range(SUB):
+                row = group * SUB + r
+                shift = jnp.broadcast_to(field[pl.ds(row, 1), :], (SUB, LANES))
+                own_image[row] = own_image[row] + own_slope[row] * shift
+            return 0
+
+        lax.fori_loop(cut * (groups // CUTS), (cut + 1) * (groups // CUTS), body, 0, unroll=2)
+        save(cut).start()
+    for cut in range(CUTS):
+        save(cut).wait()
 
 
 def per_device(images, gradient, shifts, tile_blocks, intersections, start_coefficients):
@@ -661,7 +734,7 @@
     pair_of = pltpu.SemaphoreType.DMA((2,))
     chunk_of = pltpu.SemaphoreType.DMA((CHUNKS,))
 
-    basis, weight, pull, below, above, factors, chosen, coef, local = pl.pallas_call(
+    basis, weight, pull, below, above, bands, chosen, coef, local = pl.pallas_call(
         functools.partial(
             begin_kernel, depth, plane, block, tile_count, knot_count, cap, wide
         ),
@@ -671,7 +744,7 @@
             f32(rows, LANES),
             f32(rows, SUB, LANES),
             f32(rows, SUB, LANES),
-            f32(4, block, SUB, LANES),
+            f32(tile_count, SUB, LANES),
             f32(2 * tile_count, LANES),
             f32(block, LANES),
             f32(knots + SUB, LANES),
@@ -685,11 +758,17 @@
             pltpu.VMEM((3, 2 * cap, LANES), jnp.float32),
             pltpu.VMEM((2, 2 * cap, LANES), jnp.float32),
             pltpu.VMEM((BAND, knots + SUB, SUB, LANES), jnp.float32),
-            pltpu.VMEM((BAND, block, LANES), jnp.float32),
-            pltpu.VMEM((2 * SUB, LANES), jnp.float32),
+            pltpu.VMEM((SUB, LANES), jnp.float32),
+            pltpu.VMEM((SUB, LANES), jnp.float32),
+            pltpu.VMEM((tile_count, SUB, LANES), jnp.float32),
+            pltpu.VMEM((knot_count, tile_count, SUB, LANES), jnp.float32),
             pair_of, pair_of, pair_of, pair_of, pair_of,
             chunk_of, chunk_of, chunk_of, chunk_of,
-            *share_scratch(tile_count, knot_count, 2 * SUB),
+            pltpu.SemaphoreType.DMA((tile_count,)),
+            pltpu.SemaphoreType.DMA((tile_count,)),
+            pltpu.SemaphoreType.DMA((knot_count,)),
+            pltpu.SemaphoreType.DMA((knot_count,)),
+            *share_scratch(tile_count, knot_count, SUB),
         ],
         compiler_params=pltpu.CompilerParams(
             collective_id=0, has_side_effects=True, vmem_limit_bytes=48 * 1024 * 1024
@@ -702,55 +781,64 @@
         in_specs=[SMEM] + [ANY] * 4,
         out_specs=(VMEM,) * 2,
         scratch_shapes=[volume] * 4 + [pltpu.SemaphoreType.DMA((4,))],
-        compiler_params=pltpu.CompilerParams(vmem_limit_bytes=48 * 1024 * 1024),
+        compiler_params=pltpu.CompilerParams(vmem_limit_bytes=16 * 1024 * 1024),
         name="pairs",
     )(intersections, image, slope, below, above)
     penalty = jnp.asarray(smoothing(block))
 
+    factors = bands
     for step in range(ITERS):
-        grads = pl.pallas_call(
+        opening = step == 0
+        landed = pl.pallas_call(
             functools.partial(project_kernel, plane, knots, cap),
-            out_shape=f32(SUB, LANES),
+            out_shape=f32(3, padded, LANES),
             in_specs=[SMEM] * 2 + [VMEM] * 6,
             out_specs=VMEM,
             scratch_shapes=[
                 pltpu.VMEM((padded, LANES), jnp.float32),
-                pltpu.VMEM((3, padded, LANES), jnp.float32),
                 pltpu.VMEM((2, (SPAN + 3) * SUB, LANES), jnp.float32),
             ],
             compiler_params=PARAMS,
             name="project",
         )(intersections, shifts, local, basis, weight, pull, image_sum, slope_sum)
-        coef, local, own = pl.pallas_call(
-            functools.partial(settle_kernel, tile_count, knot_count, block),
-            out_shape=(f32(block, LANES), f32(knots + SUB, LANES), f32(SUB, block)),
-            in_specs=[SMEM] + [VMEM] * 5,
-            out_specs=(VMEM,) * 3,
+        outs = (f32(block, LANES), f32(knots + SUB, LANES), f32(SUB, block))
+        if opening:
+            outs += (f32(4, block, SUB, LANES),)
+        coef, local, own, *made = pl.pallas_call(
+            functools.partial(settle_kernel, tile_count, knot_count, block, plane, opening),
+            out_shape=outs,
+            in_specs=[SMEM] + [VMEM] * 6,
+            out_specs=(VMEM,) * len(outs),
             scratch_shapes=[
                 pltpu.VMEM((block, LANES), jnp.float32),
+                pltpu.VMEM((SUB, LANES), jnp.float32),
+                *([pltpu.VMEM((BAND, block, LANES), jnp.float32)] if opening else []),
                 *share_scratch(tile_count, knot_count, SUB),
             ],
             compiler_params=pltpu.CompilerParams(
-                collective_id=1, has_side_effects=True, vmem_limit_bytes=16 * 1024 * 1024
+                collective_id=1 if opening else 2,
+                has_side_effects=True,
+                vmem_limit_bytes=16 * 1024 * 1024,
             ),
-            name="settle",
-        )(tile_blocks, grads, chosen, factors, coef, penalty)
-
-    cuts = 8
-    part = pl.BlockSpec((rows // cuts, SUB, LANES), lambda i: (i, 0, 0))
+            name="settle_first" if opening else "settle",
+        )(tile_blocks, landed, basis, chosen, factors, coef, penalty)
+        if opening:
+            factors = made[0]
+
+    whole = pltpu.VMEM((rows, SUB, LANES), jnp.float32)
     warped = pl.pallas_call(
-        functools.partial(warp_kernel, plane, knots, depth),
+        functools.partial(warp_kernel, plane, knots),
         out_shape=f32(rows, depth, LANES),
-        grid=(cuts,),
-        in_specs=[
-            SMEM,
-            pl.BlockSpec((knots + SUB, LANES), lambda i: (0, 0)),
-            pl.BlockSpec((groups * WINDOW // cuts, SUB, LANES), lambda i: (i, 0, 0)),
-            part,
-            part,
+        in_specs=[SMEM, VMEM, VMEM, ANY, ANY],
+        out_specs=ANY,
+        scratch_shapes=[
+            whole,
+            whole,
+            pltpu.VMEM((rows, LANES), jnp.float32),
+            pltpu.SemaphoreType.DMA((2, CUTS)),
+            pltpu.SemaphoreType.DMA((CUTS,)),
         ],
-        out_specs=part,
-        compiler_params=pltpu.CompilerParams(vmem_limit_bytes=56 * 1024 * 1024),
+        compiler_params=PARAMS,
         name="warp",
     )(shifts, local, basis, image, slope)
     return own[0:1], warped.transpose(1, 0, 2).reshape(1, depth, plane)

time: 93.9 us -> 86.2 us (0.918)
  Pallas kernels: 87.6 us -> 80.4 us
    pallas_call x1, Pallas kernels: 6.66 us -> 2 us  [per_device(): pl.pallas_call(functools.partial(warp_kernel, plane, knots), out_shape=f3...]
    pallas_call x2, Pallas kernels: 7.9 us -> 6.42 us  [per_device(): pl.pallas_call(functools.partial(project_kernel, plane, knots, cap), out_...]
    pallas_call x1, Pallas kernels: 46 us -> 44.8 us  [per_device(): pl.pallas_call(functools.partial(begin_kernel, depth, plane, block, tile_...]
    unnamed x17 -> x13, local copies, waits for them, and re-layouts: 4.04 us -> 3.69 us
where the time goes in v3:
time: 86.2 us; the launch traced here: 86 us
  Pallas kernels  80.4 us (93%)
  local copies, waits for them, and re-layouts  4.2 us (5%)
  between operations  1.38 us (2%)
    pallas_call x1, Pallas kernels, per_device(): pl.pallas_call(functools.partial(begin_kernel, depth, plane, block, tile_...  44.8 us
    pallas_call x2, Pallas kernels, per_device(): pl.pallas_call(functools.partial(settle_kernel, tile_count, knot_count, b...  21.7 us
    pallas_call x2, Pallas kernels, per_device(): pl.pallas_call(functools.partial(project_kernel, plane, knots, cap), out_...  6.42 us
    pallas_call x1, Pallas kernels, per_device(): pl.pallas_call(functools.partial(pair_kernel, rows, cap), out_shape=(f32(...  5.45 us
    unnamed x13, local copies, waits for them, and re-layouts  3.69 us
    pallas_call x1, Pallas kernels, per_device(): pl.pallas_call(functools.partial(warp_kernel, plane, knots), out_shape=f3...  2 us

profile of v3, /device:TPU:0, one launch (start us, length us, event | category | flops | bytes accessed | tf_op | source)
XLA Modules:
  0.0 86.0 jit_solution(199092526301683077)
XLA Ops:
  0.6 0.8 copy.12.table
  1.4 0.0 copy-start.4
  1.4 0.7 copy-done.4
  2.1 0.0 copy-start.5
  2.1 0.7 copy-done.5
  2.7 0.0 copy-start
  2.7 0.0 copy-start.1
  2.7 44.8 %begin.1 = (f32[384,8,128]{2,1,0:T(8,128)S(1)}, f32[512,128]{1,0:T(8,128)S(1)}, f32[512,128]{1,0:T(8,128)S(1)}, f32[512,8,128]{2,1,0:T(8,128)S(1)}, f32[512,8,12...) custom-call(s32[1,2]{1,0:T(1,128)S(1)} %copy-done.4, ...), custom_call_target="tpu_custom_call" | custom-call | tf_op jit(solution)/shard_map/begin/pallas_call | solution.py:737
  47.5 0.0 copy-done
  47.5 0.0 copy-done.1
  47.5 0.0 copy-start.2
  47.6 1.6 %copy-done.2 = f32[512,8,128]{2,1,0:T(8,128)S(1)} copy-done((f32[512,8,128]{2,1,0:T(8,128)S(1)}, f32[512,8,128]{2,1,0:T(8,128)}, u32[]{:S(2)}) %copy-start.2) | copy-done | bytes 2097176
  49.1 5.5 %pairs.1 = (f32[24,72,128]{2,1,0:T(8,128)S(1)}, f32[24,72,128]{2,1,0:T(8,128)S(1)}) custom-call(s32[1,3,8,5]{3,2,1,0:T(8,128)S(1)} %copy.12.table, f32[512,8,128]{2,1,0:T(8,128)S(1)} %bitcast.10, f32[512,8,128]{2,1,0:T(8,128)S(1)} %bitcast.13, f32[512,8,128]{2,1,0:T(8,128)S(1)} %get-tuple-element.22.below, f32[512,8,128]{2,1,0:T(8,128)S(1)} %copy-done.2), custom_call_target="tpu_custom_call" | custom-call | tf_op jit(solution)/shard_map/pairs/pallas_call | solution.py:778
  55.2 0.0 copy-start.3
  55.3 3.2 %project.2.landed = f32[3,536,128]{2,1,0:T(8,128)S(1)} custom-call(s32[1,3,8,5]{3,2,1,0:T(8,128)S(1)} %copy.12.table, s32[1]{0:T(128)S(6)} %copy.13.rigid, f32[136,128]{1,0:T(8,128)S(1)} %get-tuple-element.18.local, f32[384,8,128]{2,1,0:T(8,128)S(1)} %get-tuple-element.19.basis, f32[512,128]{1,0:T(8,128)S(1)} %get-tuple-element.20.weight, ...), custom_call_target="tpu_custom_call" | custom-call | tf_op jit(solution)/shard_map/project/pallas_call | solution.py:792
  58.5 0.0 copy-done.3
  58.5 10.0 %settle_first.1 = (f32[64,128]{1,0:T(8,128)S(1)}, f32[136,128]{1,0:T(8,128)S(1)}, f32[8,64]{1,0:T(8,128)}, f32[4,64,8,128]{3,2,1,0:T(8,128)S(1)}) custom-call(s32[1,2]{1,0:T(1,128)S(1)} %copy-done.4, f32[3,536,128]{2,1,0:T(8,128)S(1)} %project.2.landed, f32[384,8,128]{2,1,0:T(8,128)S(1)} %get-tuple-element.19.basis, f32[16,128]{1,0:T(8,128)S(1)} %get-tuple-element.26.chosen, ...), custom_call_target="tpu_custom_call" | custom-call | tf_op jit(solution)/shard_map/settle_first/pallas_call | solution.py:807
  68.5 3.2 %project.3.landed = f32[3,536,128]{2,1,0:T(8,128)S(1)} custom-call(s32[1,3,8,5]{3,2,1,0:T(8,128)S(1)} %copy.12.table, s32[1]{0:T(128)S(6)} %copy.13.rigid, f32[136,128]{1,0:T(8,128)S(1)} %get-tuple-element.29.local, f32[384,8,128]{2,1,0:T(8,128)S(1)} %get-tuple-element.19.basis, f32[512,128]{1,0:T(8,128)S(1)} %get-tuple-element.20.weight, ...), custom_call_target="tpu_custom_call" | custom-call | tf_op jit(solution)/shard_map/project/pallas_call | solution.py:792
  71.7 11.7 %settle.1 = (f32[64,128]{1,0:T(8,128)}, f32[136,128]{1,0:T(8,128)S(1)}, f32[8,64]{1,0:T(8,128)S(1)}) custom-call(s32[1,2]{1,0:T(1,128)S(1)} %copy-done.4, f32[3,536,128]{2,1,0:T(8,128)S(1)} %project.3.landed, f32[384,8,128]{2,1,0:T(8,128)S(1)} %get-tuple-element.19.basis, f32[16,128]{1,0:T(8,128)S(1)} %get-tuple-element.26.chosen, ...), custom_call_target="tpu_custom_call" | custom-call | tf_op jit(solution)/shard_map/settle/pallas_call | solution.py:807
  83.4 2.0 %warp.1 = f32[512,8,128]{2,1,0:T(8,128)} custom-call(s32[1]{0:T(128)S(6)} %copy.13.rigid, f32[136,128]{1,0:T(8,128)S(1)} %get-tuple-element.33.local, f32[384,8,128]{2,1,0:T(8,128)S(1)} %get-tuple-element.19.basis, f32[512,8,128]{2,1,0:T(8,128)S(1)} %bitcast.11, f32[512,8,128]{2,1,0:T(8,128)S(1)} %bitcast.14), custom_call_target="tpu_custom_call" | custom-call | tf_op jit(solution)/shard_map/warp/pallas_call | solution.py:829
  85.4 0.5 slice.3
Async XLA Ops:
  1.4 0.7 copy-start.4
  2.1 0.7 copy-start.5
  2.7 44.8 %copy-start = (f32[1,8,65536]{2,1,0:T(8,128)S(1)}, f32[1,8,65536]{2,1,0:T(8,128)}, u32[]{:S(2)}) copy-start(f32[1,8,65536]{2,1,0:T(8,128)} %param.7) | copy-start | bytes 6291460
  2.7 44.8 %copy-start.1 = (f32[1,8,65536]{2,1,0:T(8,128)S(1)}, f32[1,8,65536]{2,1,0:T(8,128)}, u32[]{:S(2)}) copy-start(f32[1,8,65536]{2,1,0:T(8,128)} %param.8) | copy-start | bytes 6291460
  47.5 1.6 %copy-start.2 = (f32[512,8,128]{2,1,0:T(8,128)S(1)}, f32[512,8,128]{2,1,0:T(8,128)}, u32[]{:S(2)}) copy-start(f32[512,8,128]{2,1,0:T(8,128)} %get-tuple-element.23.above) | copy-start | bytes 6291460
  55.2 3.2 %copy-start.3 = (f32[64,64]{1,0:T(8,128)S(1)}, f32[64,64]{1,0:T(8,128)}, u32[]{:S(2)}) copy-start(f32[64,64]{1,0:T(8,128)} %constant.2.clone.penalty) | copy-start | bytes 49156

commit v4 on v3

--- a/solution.py
+++ b/solution.py
@@ -19,6 +19,8 @@
 WINDOW = 6
 BAND = 4
 CHUNKS = 4
+REACH = WINDOW + 1
+SPOTS = 24
 CUTS = 8
 SPAN = SLAB // GROUP + 1
 
@@ -56,6 +58,13 @@
         left, right, (((1,), (1,)), ((), ())), precision=HIGHEST,
         preferred_element_type=jnp.float32,
     )
+
+
+def spline(offset):
+    dist = jnp.abs(offset)
+    inner = 2.0 / 3.0 - dist * dist + 0.5 * dist * dist * dist
+    outer = (2.0 - dist) * (2.0 - dist) * (2.0 - dist) * (1.0 / 6.0)
+    return jnp.where(dist < 1.0, inner, jnp.where(dist < 2.0, outer, 0.0))
 
 
 def grid_iota():
@@ -123,7 +132,7 @@
     ]
 
 
-def share(tile_count, knot_count, mine, scratch, between=None):
+def share(tile_count, knot_count, mine, scratch):
     total, column, table, send_a, recv_a, send_b, recv_b = scratch
     tile, knot = lax.axis_index("tile"), lax.axis_index("knot")
 
@@ -147,41 +156,32 @@
             device_id_type=MESH,
         )
 
-    for step in range(1, knot_count):
-        over_knot(step, knot).start()
-    column[knot] = mine[...]
-    if between is not None:
-        between()
-    for step in range(1, knot_count):
-        over_knot(step, lax.rem(knot + step, knot_count)).wait_recv()
-    total[...] = jnp.sum(column[...], axis=0)
-
-    def send(step, _):
-        over_tile(step, tile).start()
-        return 0
-
-    lax.fori_loop(1, tile_count, send, 0)
-    table[tile] = total[...]
+    def each(count, act):
+        def body(step, _):
+            act(step)
+            return 0
+
+        lax.fori_loop(1, count, body, 0)
+
+    def open_knot():
+        each(knot_count, lambda step: over_knot(step, knot).start())
+        column[knot] = mine[...]
+
+    def open_tile():
+        each(knot_count, lambda step: over_knot(step, lax.rem(knot + step, knot_count)).wait_recv())
+        total[...] = jnp.sum(column[...], axis=0)
+        each(tile_count, lambda step: over_tile(step, tile).start())
+        table[tile] = total[...]
 
     def arrived():
-        def arrive(step, _):
-            over_tile(step, lax.rem(tile + step, tile_count)).wait_recv()
-            return 0
-
-        lax.fori_loop(1, tile_count, arrive, 0)
-        return table
+        each(tile_count, lambda step: over_tile(step, lax.rem(tile + step, tile_count)).wait_recv())
+        return table[...]
 
     def finish():
-        for step in range(1, knot_count):
-            over_knot(step, knot).wait_send()
-
-        def sent(step, _):
-            over_tile(step, tile).wait_send()
-            return 0
-
-        lax.fori_loop(1, tile_count, sent, 0)
-
-    return arrived, finish
+        each(knot_count, lambda step: over_knot(step, knot).wait_send())
+        each(tile_count, lambda step: over_tile(step, tile).wait_send())
+
+    return open_knot, open_tile, arrived, finish
 
 
 def halves(value, block):
@@ -281,11 +281,10 @@
 def begin_kernel(
     depth, plane, block, tile_count, knot_count, cap, wide,
     blocks, table, first_coef, image, slope,
-    basis, weight, pull, below, above, bands, chosen, coef, local,
-    own_image, own_slope, passing, tabs, tabs_in, acc, mine, first, heads, columns,
+    basis, weight, pull, below, above, bands, chosen, coef, local, shapes, spots,
+    own_image, own_slope, passing, tabs, tabs_in, acc, first, heads, columns,
     here_sem, tab_send, tab_recv, big_send, big_recv, chunk_send, chunk_recv, pass_send, pass_recv,
     head_send, head_recv, column_send, column_recv,
-    *share_refs,
 ):
     knots = 2 * block
     rows = plane // LANES
@@ -351,10 +350,10 @@
             tile + (1 - 2 * side),
         )
 
-    def direct(side, count):
+    def direct(side, c):
         return remote(
-            slope.at[pl.ds(0, count)], land[side].at[pl.ds(0, count)],
-            big_send.at[side], big_recv.at[side], tile + (1 - 2 * side),
+            slope.at[pl.ds(c * piece, piece)], land[side].at[pl.ds(c * piece, piece)],
+            big_send.at[side, c], big_recv.at[side, c], tile + (1 - 2 * side),
         )
 
     def to_relay(side, c):
@@ -386,19 +385,34 @@
     for side in range(2):
         when(goes[side])(lambda side=side: tab_copy(side).start())
     each(tile_count, lambda step: head_copy(step, tile).start())
-    for side in range(2):
-        if wide:
-            def split(side=side):
-                for c in range(CHUNKS):
-                    to_relay(side, c).start()
-                direct(side, half).start()
-
-            when(goes[side], edge_out[side])(split)
-            when(goes[side], jnp.logical_not(edge_out[side]))(
-                lambda side=side: direct(side, rows).start()
-            )
-        else:
-            when(goes[side])(lambda side=side: direct(side, rows).start())
+    def for_pieces(order, flags, edges, plain, relayed):
+        for c in order:
+            for side in range(2):
+                if wide and c >= CHUNKS:
+                    when(flags[side], edges[side])(
+                        lambda side=side, c=c: relayed(side, c - CHUNKS)
+                    )
+                    when(flags[side], jnp.logical_not(edges[side]))(
+                        lambda side=side, c=c: plain(side, c)
+                    )
+                else:
+                    when(flags[side])(lambda side=side, c=c: plain(side, c))
+
+    order = [c for pair in zip(range(CHUNKS, 2 * CHUNKS), range(CHUNKS)) for c in pair]
+    edges = edge_out if wide else None
+
+    def launch(part):
+        for_pieces(
+            part, goes, edges,
+            lambda side, c: direct(side, c).start(),
+            lambda side, c: to_relay(side, c).start(),
+        )
+
+    launch(order[:2])
+    each(tile_count, lambda step: head_copy(step, lax.rem(tile + step, tile_count)).wait_recv())
+    each(knot_count, lambda step: column_copy(step, knot).start())
+    launch(order[2:])
+    columns[knot] = heads[...]
 
     def forward(c):
         if wide:
@@ -451,10 +465,7 @@
         place = at * ((knots - 3) / plane) + 1.0
         parts = []
         for i in range(WINDOW):
-            dist = jnp.abs(place - (knot0 + i).astype(jnp.float32))
-            inner = 2.0 / 3.0 - dist * dist + 0.5 * dist * dist * dist
-            outer = (2.0 - dist) * (2.0 - dist) * (2.0 - dist) * (1.0 / 6.0)
-            value = jnp.where(dist < 1.0, inner, jnp.where(dist < 2.0, outer, 0.0))
+            value = spline(place - (knot0 + i).astype(jnp.float32))
             basis[group * WINDOW + i] = value
             parts.append(value)
         for i in range(WINDOW):
@@ -467,14 +478,10 @@
     forward(1)
     lax.fori_loop(groups // 2, groups, body, 0)
     forward(2)
-    clear(mine)
     for d in range(BAND):
-        mine[d : d + 1, :] = lane_sums(acc[d, 0:knots])
-    each(tile_count, lambda step: head_copy(step, lax.rem(tile + step, tile_count)).wait_recv())
-    each(knot_count, lambda step: column_copy(step, knot).start())
-    columns[knot] = heads[...]
+        bands[d : d + 1, :] = lane_sums(acc[d, 0:knots])
+    bands[BAND:SUB, :] = jnp.zeros((SUB - BAND, LANES), jnp.float32)
     forward(3)
-    arrived, finish = share(tile_count, knot_count, mine, share_refs)
     each(
         knot_count,
         lambda step: column_copy(step, lax.rem(knot + step, knot_count)).wait_recv(),
@@ -491,43 +498,49 @@
     coef[...] = start
     spread_coef(blocks, start, local)
 
-    for side in range(2):
-        if wide:
-            def pieces(side=side):
-                direct(side, half).wait_recv()
-                for c in range(CHUNKS):
-                    from_relay(side, c).wait_recv()
-
-            when(comes[side], edge_in[side])(pieces)
-            when(comes[side], jnp.logical_not(edge_in[side]))(
-                lambda side=side: direct(side, rows).wait_recv()
-            )
-        else:
-            when(comes[side])(lambda side=side: direct(side, rows).wait_recv())
-    bands[...] = arrived()[...]
-    finish()
+    for d in range(3):
+
+        def shape(m, _):
+            at_pair = d * cap + m
+            low = table[0, d, m, 1] & (GROUP - 1)
+            origin = table[0, d, m, 3] - low
+            knot0 = (origin * (knots - 3)) >> (plane.bit_length() - 1)
+            place = (place0 + origin).astype(jnp.float32)
+            for i in range(SPAN):
+                here = (place + float(i * GROUP)) * ((knots - 3) / plane) + 1.0
+                for r in range(REACH):
+                    j = knot0 + (i * GROUP * (knots - 3) // plane + r)
+                    shapes[at_pair, i * REACH + r] = spline(here - j.astype(jnp.float32))
+            row = lax.broadcasted_iota(jnp.int32, (SPOTS, LANES), 0)
+            col = lax.broadcasted_iota(jnp.int32, (SPOTS, LANES), 1)
+            spots[pl.ds(pl.multiple_of(at_pair * SPOTS, SUB), SPOTS), :] = (
+                row + knot0 == col
+            ).astype(jnp.float32)
+            return 0
+
+        lax.fori_loop(0, cap, shape, 0)
+
+    for_pieces(
+        order, comes, edge_in if wide else None,
+        lambda side, c: direct(side, c).wait_recv(),
+        lambda side, c: from_relay(side, c).wait_recv(),
+    )
     each(tile_count, lambda step: head_copy(step, tile).wait_send())
     each(knot_count, lambda step: column_copy(step, knot).wait_send())
     for side in range(2):
         when(goes[side])(lambda side=side: tab_copy(side).wait_send())
-        if wide:
-            def sent(side=side):
-                for c in range(CHUNKS):
-                    to_relay(side, c).wait_send()
-                direct(side, half).wait_send()
-
-            when(goes[side], edge_out[side])(sent)
-            when(goes[side], jnp.logical_not(edge_out[side]))(
-                lambda side=side: direct(side, rows).wait_send()
-            )
-
+    for_pieces(
+        order, goes, edges,
+        lambda side, c: direct(side, c).wait_send(),
+        lambda side, c: to_relay(side, c).wait_send(),
+    )
+    if wide:
+        for side in range(2):
             def passed(side=side):
                 for c in range(CHUNKS):
                     from_relay(side, c).wait_send()
 
             when(relays[side])(passed)
-        else:
-            when(goes[side])(lambda side=side: direct(side, rows).wait_send())
 
 
 def fill_field(groups, plane, knots, base, local, basis, store):
@@ -539,136 +552,146 @@
         store(group, value + base)
 
 
-def project_kernel(
-    plane, knots, cap, table, rigid, local, basis, weight, pull, image_sum, slope_sum,
-    landed, field, moved,
+def refine_kernel(
+    plane, tile_count, knot_count, block, cap,
+    blocks, table, rigid, basis, weight, pull, image_sum, slope_sum, shapes, spots, bands, chosen,
+    coef_in, local_in, penalty, local, own_out,
+    field, coef, factors, system, work, marks, mine_first, mine_second, *share_refs,
 ):
+    knots = 2 * block
     groups = plane // GROUP
-    rows = plane // LANES
-    sub, lane = grid_iota()
-    field[0:FRONT, :] = jnp.zeros((FRONT, LANES), jnp.float32)
-    field[FRONT + rows : FRONT + rows + BACK, :] = jnp.zeros((BACK, LANES), jnp.float32)
-    clear(landed)
-    clear(moved)
+    each = len(share_refs) // 3
+    sets = [share_refs[n * each : (n + 1) * each] for n in range(3)]
+    field[groups] = jnp.zeros((SUB, LANES), jnp.float32)
     base = shift_step * rigid[0].astype(jnp.float32)
-
-    def store(group, value):
-        field[FRONT + group * SUB : FRONT + (group + 1) * SUB, :] = value
-
-    fill_field(groups, plane, knots, base, local, basis, store)
-
-    for side in range(3):
-
-        def body(pair, _):
-            at_pair = side * cap + pair
-            low, row_b, row_a, turn = pair_place(table, side, pair)
-            keep = lane < LANES - turn
-            slot = pair & 1
-            for i in range(SPAN):
-                at = pl.ds(pl.multiple_of(row_b + i * SUB, SUB), SUB)
-                here = pl.ds(i * SUB, SUB)
-                moved[slot, pl.ds(SUB + i * SUB, SUB), :] = (
-                    image_sum[at_pair, here, :] + field[at, :] * slope_sum[at_pair, here, :]
-                )
-            for i in range(SPAN + 1):
-                term = jnp.where(
-                    keep,
-                    moved[slot, pl.ds(SUB + i * SUB, SUB), :],
-                    moved[slot, pl.ds(SUB + i * SUB - 1, SUB), :],
-                )
-                landed[side, pl.ds(row_a + i * SUB, SUB), :] += pltpu.roll(term, turn, 1)
-            return 0
-
-        lax.fori_loop(0, cap, body, 0)
-
-    def own(group, _):
-        at = pl.ds(pl.multiple_of(FRONT + group * SUB, SUB), SUB)
-        here = pl.ds(pl.multiple_of(group * SUB, SUB), SUB)
-        landed[1, at, :] = landed[1, at, :] - pull[here, :] - weight[here, :] * field[at, :]
-        return 0
-
-    lax.fori_loop(0, groups, own, 0, unroll=4)
-
-
-def project(groups, plane, knots, basis, landed, grads):
+    ones = jnp.ones((SUB, LANES), jnp.float32)
+    local[...] = local_in[...]
+    coef[...] = coef_in[...]
     holders = [[] for _ in range(knots)]
     for group in range(groups):
         first = group * GROUP * (knots - 3) // plane
         for i in range(WINDOW):
             if first + i < knots:
                 holders[first + i].append((group, group * WINDOW + i))
-    for q, side in enumerate((1, 0, 2)):
+
+    def store(group, value):
+        field[group] = value
+
+    def slabs():
+        fill_field(groups, plane, knots, base, local, basis, store)
+        for side in range(3):
+
+            def body(m, _):
+                pair = side * cap + m
+                group = lax.shift_right_logical(table[0, side, m, 1], GROUP.bit_length() - 1)
+                parts = [None] * SPOTS
+                for i in range(SPAN):
+                    here = pl.ds(i * SUB, SUB)
+                    term = image_sum[pair, here, :] + slope_sum[pair, here, :] * field[group + i]
+                    for r in range(REACH):
+                        j = i * GROUP * (knots - 3) // plane + r
+                        value = term * shapes[pair, i * REACH + r]
+                        parts[j] = value if parts[j] is None else parts[j] + value
+                zero = jnp.zeros((SUB, LANES), jnp.float32)
+                parts = [zero if part is None else part for part in parts]
+                for j in range(0, SPOTS, SUB):
+                    marks[pl.ds(pl.multiple_of(pair * SPOTS + j, SUB), SUB), :] = row_sums(
+                        parts[j : j + SUB]
+                    )
+                return 0
+
+            lax.fori_loop(0, cap, body, 0)
+
+    def gather(mine):
+        for group in range(groups):
+            here = slice(group * SUB, (group + 1) * SUB)
+            field[group] = pull[here, :] + weight[here, :] * field[group]
         parts = []
         for j in range(knots):
             total = None
             for group, at in holders[j]:
-                term = basis[at] * landed[side, FRONT + group * SUB : FRONT + (group + 1) * SUB, :]
+                term = basis[at] * field[group]
                 total = term if total is None else total + term
             parts.append(total)
-        parts = [row_sums(parts[j : j + SUB]) for j in range(0, knots, SUB)]
-        sums = jnp.concatenate(parts, axis=0)
-        line = lanes_dot(jnp.ones((SUB, LANES), jnp.float32), sums)
-        grads[q : q + 1, :] = -line[0:1, :]
-    grads[3:SUB, :] = jnp.zeros((SUB - 3, LANES), jnp.float32)
-
-
-def settle_kernel(
-    tile_count, knot_count, block, plane, opening, blocks, landed, basis, chosen, given, coef,
-    penalty, coef_out, local, own_out, *refs,
-):
-    if opening:
-        factors, work, mine, system, *share_refs = refs
-    else:
-        factors, (work, mine, *share_refs) = given, refs
-
-    def gather():
-        project(plane // GROUP, plane, 2 * block, basis, landed, mine)
-
-    def prepare():
-        if opening:
-            select = chosen[...]
-            bands = given[...]
-            for d in range(BAND):
-                system[d] = cols_dot(halves(bands[:, d, :], block), select)
-            factor(block, smoothing(block), system, factors)
-
-    greet(tile_count, knot_count, gather)
-    arrived, finish = share(tile_count, knot_count, mine, share_refs, prepare)
-    sums = arrived()[...]
-    own, lower, upper = sums[:, 0, :], sums[:, 1, :], sums[:, 2, :]
-    none = jnp.zeros((1, LANES), jnp.float32)
-    grads = (
-        own
-        + jnp.concatenate([lower[1:, :], none], axis=0)
-        + jnp.concatenate([none, upper[:-1, :]], axis=0)
-    )
-    grad_sum = cols_dot(halves(grads, block), chosen[...])
-    bend = jnp.dot(
-        penalty[...], coef[...], precision=HIGHEST, preferred_element_type=jnp.float32
-    )
-    work[...] = -(grad_sum + smooth_weight * bend)
-    forward = []
-    for k in range(block):
-        value = spread(work, k)
-        for back in (3, 2, 1):
-            if k >= back:
-                value = value - factors[back - 1, k] * forward[k - back]
-        forward.append(value)
-    steps = [None] * block
-    for k in reversed(range(block)):
-        value = forward[k] * factors[3, k]
-        for ahead in (3, 2, 1):
-            if k + ahead < block:
-                value = value - factors[ahead - 1, k + ahead] * steps[k + ahead]
-        steps[k] = value
-        work[k : k + 1, :] = value[0:1, :]
-    fresh = coef[...] + work[...]
-    coef_out[...] = fresh
-    spread_coef(blocks, fresh, local)
+        sums = jnp.concatenate(
+            [row_sums(parts[j : j + SUB]) for j in range(0, knots, SUB)], axis=0
+        )
+        count = cap * SPOTS
+        lines = []
+        for side in range(3):
+            at = slice(side * count, (side + 1) * count)
+            values = lanes_dot(ones, marks[at, :])
+            lines.append(
+                -jnp.dot(
+                    values, spots[at, :], precision=HIGHEST, preferred_element_type=jnp.float32
+                )[0:1, :]
+            )
+        mine[0:1, :] = lanes_dot(ones, sums)[0:1, :] + lines[1]
+        mine[1:2, :] = lines[0]
+        mine[2:3, :] = lines[2]
+        mine[3:SUB, :] = jnp.zeros((SUB - 3, LANES), jnp.float32)
+
+    def solve(sums):
+        own, lower, upper = sums[:, 0, :], sums[:, 1, :], sums[:, 2, :]
+        none = jnp.zeros((1, LANES), jnp.float32)
+        grads = (
+            own
+            + jnp.concatenate([lower[1:, :], none], axis=0)
+            + jnp.concatenate([none, upper[:-1, :]], axis=0)
+        )
+        grad_sum = cols_dot(halves(grads, block), chosen[...])
+        bend = jnp.dot(
+            penalty[...], coef[...], precision=HIGHEST, preferred_element_type=jnp.float32
+        )
+        work[...] = -(grad_sum + smooth_weight * bend)
+        forward = []
+        for k in range(block):
+            value = spread(work, k)
+            for back in (3, 2, 1):
+                if k >= back:
+                    value = value - factors[back - 1, k] * forward[k - back]
+            forward.append(value)
+        steps = [None] * block
+        for k in reversed(range(block)):
+            value = forward[k] * factors[3, k]
+            for ahead in (3, 2, 1):
+                if k + ahead < block:
+                    value = value - factors[ahead - 1, k + ahead] * steps[k + ahead]
+            steps[k] = value
+            work[k : k + 1, :] = value[0:1, :]
+        coef[...] = coef[...] + work[...]
+        spread_coef(blocks, coef[...], local)
+
+    greet(tile_count, knot_count, slabs)
+    band_knot, band_tile, band_table, band_finish = share(tile_count, knot_count, bands, sets[0])
+    band_knot()
+    open_knot, open_tile, arrived, finish_first = share(
+        tile_count, knot_count, mine_first, sets[1]
+    )
+    gather(mine_first)
+    open_knot()
+    band_tile()
+    open_tile()
+    table_of = band_table()
+    select = chosen[...]
+    for d in range(BAND):
+        system[d] = cols_dot(halves(table_of[:, d, :], block), select)
+    factor(block, smoothing(block), system, factors)
+    solve(arrived())
+    slabs()
+    gather(mine_second)
+    open_knot, open_tile, arrived, finish_second = share(
+        tile_count, knot_count, mine_second, sets[2]
+    )
+    open_knot()
+    open_tile()
+    solve(arrived())
     lane = lax.broadcasted_iota(jnp.int32, (SUB, LANES), 1)
     me = lax.axis_index("tile") * knot_count + lax.axis_index("knot")
-    own_out[...] = lanes_dot((lane == me).astype(jnp.float32), fresh)
-    finish()
+    own_out[...] = lanes_dot((lane == me).astype(jnp.float32), coef[...])
+    band_finish()
+    finish_first()
+    finish_second()
 
 
 def warp_kernel(
@@ -732,9 +755,10 @@
     image, slope = flat(images[0]), flat(gradient[0])
     volume = pltpu.VMEM((padded, SUB, LANES), jnp.float32)
     pair_of = pltpu.SemaphoreType.DMA((2,))
+    piece_of = pltpu.SemaphoreType.DMA((2, 2 * CHUNKS))
     chunk_of = pltpu.SemaphoreType.DMA((CHUNKS,))
 
-    basis, weight, pull, below, above, bands, chosen, coef, local = pl.pallas_call(
+    basis, weight, pull, below, above, bands, chosen, coef, local, shapes, spots = pl.pallas_call(
         functools.partial(
             begin_kernel, depth, plane, block, tile_count, knot_count, cap, wide
         ),
@@ -744,13 +768,15 @@
             f32(rows, LANES),
             f32(rows, SUB, LANES),
             f32(rows, SUB, LANES),
-            f32(tile_count, SUB, LANES),
+            f32(SUB, LANES),
             f32(2 * tile_count, LANES),
             f32(block, LANES),
             f32(knots + SUB, LANES),
+            f32(3 * cap, SPAN * REACH, SUB, LANES),
+            f32(3 * cap * SPOTS, LANES),
         ),
         in_specs=[SMEM, SMEM, VMEM, ANY, ANY],
-        out_specs=(VMEM,) * 3 + (ANY,) * 2 + (VMEM,) * 4,
+        out_specs=(VMEM,) * 3 + (ANY,) * 2 + (VMEM,) * 6,
         scratch_shapes=[
             pltpu.VMEM((rows, SUB, LANES), jnp.float32),
             pltpu.VMEM((rows, SUB, LANES), jnp.float32),
@@ -759,16 +785,14 @@
             pltpu.VMEM((2, 2 * cap, LANES), jnp.float32),
             pltpu.VMEM((BAND, knots + SUB, SUB, LANES), jnp.float32),
             pltpu.VMEM((SUB, LANES), jnp.float32),
-            pltpu.VMEM((SUB, LANES), jnp.float32),
             pltpu.VMEM((tile_count, SUB, LANES), jnp.float32),
             pltpu.VMEM((knot_count, tile_count, SUB, LANES), jnp.float32),
-            pair_of, pair_of, pair_of, pair_of, pair_of,
+            pair_of, pair_of, pair_of, piece_of, piece_of,
             chunk_of, chunk_of, chunk_of, chunk_of,
             pltpu.SemaphoreType.DMA((tile_count,)),
             pltpu.SemaphoreType.DMA((tile_count,)),
             pltpu.SemaphoreType.DMA((knot_count,)),
             pltpu.SemaphoreType.DMA((knot_count,)),
-            *share_scratch(tile_count, knot_count, SUB),
         ],
         compiler_params=pltpu.CompilerParams(
             collective_id=0, has_side_effects=True, vmem_limit_bytes=48 * 1024 * 1024
@@ -786,44 +810,31 @@
     )(intersections, image, slope, below, above)
     penalty = jnp.asarray(smoothing(block))
 
-    factors = bands
-    for step in range(ITERS):
-        opening = step == 0
-        landed = pl.pallas_call(
-            functools.partial(project_kernel, plane, knots, cap),
-            out_shape=f32(3, padded, LANES),
-            in_specs=[SMEM] * 2 + [VMEM] * 6,
-            out_specs=VMEM,
-            scratch_shapes=[
-                pltpu.VMEM((padded, LANES), jnp.float32),
-                pltpu.VMEM((2, (SPAN + 3) * SUB, LANES), jnp.float32),
-            ],
-            compiler_params=PARAMS,
-            name="project",
-        )(intersections, shifts, local, basis, weight, pull, image_sum, slope_sum)
-        outs = (f32(block, LANES), f32(knots + SUB, LANES), f32(SUB, block))
-        if opening:
-            outs += (f32(4, block, SUB, LANES),)
-        coef, local, own, *made = pl.pallas_call(
-            functools.partial(settle_kernel, tile_count, knot_count, block, plane, opening),
-            out_shape=outs,
-            in_specs=[SMEM] + [VMEM] * 6,
-            out_specs=(VMEM,) * len(outs),
-            scratch_shapes=[
-                pltpu.VMEM((block, LANES), jnp.float32),
-                pltpu.VMEM((SUB, LANES), jnp.float32),
-                *([pltpu.VMEM((BAND, block, LANES), jnp.float32)] if opening else []),
-                *share_scratch(tile_count, knot_count, SUB),
-            ],
-            compiler_params=pltpu.CompilerParams(
-                collective_id=1 if opening else 2,
-                has_side_effects=True,
-                vmem_limit_bytes=16 * 1024 * 1024,
-            ),
-            name="settle_first" if opening else "settle",
-        )(tile_blocks, landed, basis, chosen, factors, coef, penalty)
-        if opening:
-            factors = made[0]
+    local, own = pl.pallas_call(
+        functools.partial(refine_kernel, plane, tile_count, knot_count, block, cap),
+        out_shape=(f32(knots + SUB, LANES), f32(SUB, block)),
+        in_specs=[SMEM] * 3 + [VMEM] * 12,
+        out_specs=(VMEM,) * 2,
+        scratch_shapes=[
+            pltpu.VMEM((groups + 1, SUB, LANES), jnp.float32),
+            pltpu.VMEM((block, LANES), jnp.float32),
+            pltpu.VMEM((4, block, SUB, LANES), jnp.float32),
+            pltpu.VMEM((BAND, block, LANES), jnp.float32),
+            pltpu.VMEM((block, LANES), jnp.float32),
+            pltpu.VMEM((3 * cap * SPOTS, LANES), jnp.float32),
+            pltpu.VMEM((SUB, LANES), jnp.float32),
+            pltpu.VMEM((SUB, LANES), jnp.float32),
+            *(share_scratch(tile_count, knot_count, SUB) * ITERS),
+            *share_scratch(tile_count, knot_count, SUB),
+        ],
+        compiler_params=pltpu.CompilerParams(
+            collective_id=1, has_side_effects=True, vmem_limit_bytes=24 * 1024 * 1024
+        ),
+        name="refine",
+    )(
+        tile_blocks, intersections, shifts, basis, weight, pull, image_sum, slope_sum, shapes,
+        spots, bands, chosen, coef, local, penalty,
+    )
 
     whole = pltpu.VMEM((rows, SUB, LANES), jnp.float32)
     warped = pl.pallas_call(

time: 86.2 us -> 82.3 us (0.955)
  Pallas kernels: 80.4 us -> 76.5 us
    pallas_call x1, Pallas kernels: 44.8 us -> 38.9 us  [per_device(): pl.pallas_call(functools.partial(begin_kernel, depth, plane, block, tile_...]
    pallas_call x4 -> x1, Pallas kernels: 28.1 us -> 30.1 us  [per_device(): pl.pallas_call(functools.partial(refine_kernel, plane, tile_count, knot_c...]
    unnamed x13 -> x15, local copies, waits for them, and re-layouts: 3.69 us -> 3.69 us
where the time goes in v4:
time: 82.3 us; the launch traced here: 82 us
  Pallas kernels  76.5 us (93%)
  local copies, waits for them, and re-layouts  4.2 us (5%)
  between operations  1.35 us (2%)
    pallas_call x1, Pallas kernels, per_device(): pl.pallas_call(functools.partial(begin_kernel, depth, plane, block, tile_...  38.9 us
    pallas_call x1, Pallas kernels, per_device(): pl.pallas_call(functools.partial(refine_kernel, plane, tile_count, knot_c...  30.1 us
    pallas_call x1, Pallas kernels, per_device(): pl.pallas_call(functools.partial(pair_kernel, rows, cap), out_shape=(f32(...  5.45 us
    unnamed x15, local copies, waits for them, and re-layouts  3.69 us
    pallas_call x1, Pallas kernels, per_device(): pl.pallas_call(functools.partial(warp_kernel, plane, knots), out_shape=f3...  2 us

profile of v4, /device:TPU:0, one launch (start us, length us, event | category | flops | bytes accessed | tf_op | source)
XLA Modules:
  0.0 82.0 jit_solution(10368769482450788841)
XLA Ops:
  0.6 0.8 copy.11.table
  1.4 0.0 copy-start.5
  1.4 0.7 copy-done.5
  2.1 0.0 copy-start.6
  2.1 0.7 copy-done.6
  2.7 0.0 copy-start
  2.7 0.0 copy-start.1
  2.7 38.9 %begin.1 = (f32[384,8,128]{2,1,0:T(8,128)S(1)}, f32[512,128]{1,0:T(8,128)S(1)}, f32[512,128]{1,0:T(8,128)S(1)}, f32[512,8,128]{2,1,0:T(8,128)S(1)}, f32[512,8,12...) custom-call(s32[1,2]{1,0:T(1,128)S(1)} %copy-done.5, ...), custom_call_target="tpu_custom_call" | custom-call | tf_op jit(solution)/shard_map/begin/pallas_call | solution.py:761
  41.7 0.0 copy-done
  41.7 0.0 copy-done.1
  41.7 0.0 copy-start.3
  41.7 1.6 %copy-done.3 = f32[512,8,128]{2,1,0:T(8,128)S(1)} copy-done((f32[512,8,128]{2,1,0:T(8,128)S(1)}, f32[512,8,128]{2,1,0:T(8,128)}, u32[]{:S(2)}) %copy-start.3) | copy-done | bytes 2097176
  43.3 0.0 copy-start.2
  43.3 0.0 copy-start.4
  43.3 5.5 %pairs.1 = (f32[24,72,128]{2,1,0:T(8,128)S(1)}, f32[24,72,128]{2,1,0:T(8,128)S(1)}) custom-call(s32[1,3,8,5]{3,2,1,0:T(8,128)S(1)} %copy.11.table, f32[512,8,128]{2,1,0:T(8,128)S(1)} %bitcast.10, f32[512,8,128]{2,1,0:T(8,128)S(1)} %bitcast.13, f32[512,8,128]{2,1,0:T(8,128)S(1)} %get-tuple-element.20.below, f32[512,8,128]{2,1,0:T(8,128)S(1)} %copy-done.3), custom_call_target="tpu_custom_call" | custom-call | tf_op jit(solution)/shard_map/pairs/pallas_call | solution.py:802
  49.4 0.0 copy-done.2
  49.4 0.0 copy-done.4
  49.4 30.1 %refine.1 = (f32[136,128]{1,0:T(8,128)S(1)}, f32[8,64]{1,0:T(8,128)S(1)}) custom-call(s32[1,2]{1,0:T(1,128)S(1)} %copy-done.5, s32[1,3,8,5]{3,2,1,0:T(8,128)S(1)} %copy.11.table, s32[1]{0:T(128)S(6)} %copy.12.rigid, f32[384,8,128]{2,1,0:T(8,128)S(1)} %get-tuple-element.17.basis, f32[512,128]{1,0:T(8,128)S(1)} %get-tuple-element.18.weight, ...), custom_call_target="tpu_custom_call" | custom-call | tf_op jit(solution)/shard_map/refine/pallas_call | solution.py:813
  79.5 2.0 %warp.1 = f32[512,8,128]{2,1,0:T(8,128)} custom-call(s32[1]{0:T(128)S(6)} %copy.12.rigid, f32[136,128]{1,0:T(8,128)S(1)} %get-tuple-element.31.local, f32[384,8,128]{2,1,0:T(8,128)S(1)} %get-tuple-element.17.basis, f32[512,8,128]{2,1,0:T(8,128)S(1)} %bitcast.11, f32[512,8,128]{2,1,0:T(8,128)S(1)} %bitcast.14), custom_call_target="tpu_custom_call" | custom-call | tf_op jit(solution)/shard_map/warp/pallas_call | solution.py:840
  81.5 0.5 slice.3
Async XLA Ops:
  1.4 0.7 copy-start.5
  2.1 0.7 copy-start.6
  2.7 38.9 %copy-start = (f32[1,8,65536]{2,1,0:T(8,128)S(1)}, f32[1,8,65536]{2,1,0:T(8,128)}, u32[]{:S(2)}) copy-start(f32[1,8,65536]{2,1,0:T(8,128)} %param.7) | copy-start | bytes 6291460
  2.7 38.9 %copy-start.1 = (f32[1,8,65536]{2,1,0:T(8,128)S(1)}, f32[1,8,65536]{2,1,0:T(8,128)}, u32[]{:S(2)}) copy-start(f32[1,8,65536]{2,1,0:T(8,128)} %param.8) | copy-start | bytes 6291460
  41.7 1.6 %copy-start.3 = (f32[512,8,128]{2,1,0:T(8,128)S(1)}, f32[512,8,128]{2,1,0:T(8,128)}, u32[]{:S(2)}) copy-start(f32[512,8,128]{2,1,0:T(8,128)} %get-tuple-element.21.above) | copy-start | bytes 6291460
  43.3 6.1 %copy-start.2 = (f32[24,63,8,128]{3,2,1,0:T(8,128)S(1)}, f32[24,63,8,128]{3,2,1,0:T(8,128)}, u32[]{:S(2)}) copy-start(f32[24,63,8,128]{3,2,1,0:T(8,128)} %get-tuple-element.24.shapes) | copy-start | bytes 18579460
  43.3 6.1 %copy-start.4 = (f32[64,64]{1,0:T(8,128)S(1)}, f32[64,64]{1,0:T(8,128)}, u32[]{:S(2)}) copy-start(f32[64,64]{1,0:T(8,128)} %constant.2.clone.penalty) | copy-start | bytes 49156

commit v5 on v4

--- a/solution.py
+++ b/solution.py
@@ -795,7 +795,7 @@
             pltpu.SemaphoreType.DMA((knot_count,)),
         ],
         compiler_params=pltpu.CompilerParams(
-            collective_id=0, has_side_effects=True, vmem_limit_bytes=48 * 1024 * 1024
+            collective_id=0, has_side_effects=True, vmem_limit_bytes=46 * 1024 * 1024
         ),
         name="begin",
     )(tile_blocks, intersections, start_coefficients, image, slope)

time: 82.3 us -> 80.7 us (0.981)
  local copies, waits for them, and re-layouts: 4.2 us -> 2.62 us
    unnamed x15 -> x13, local copies, waits for them, and re-layouts: 3.69 us -> 2.11 us
where the time goes in v5:
time: 80.7 us; the launch traced here: 80.5 us
  Pallas kernels  76.5 us (95%)
  local copies, waits for them, and re-layouts  2.62 us (3%)
  between operations  1.36 us (2%)
    pallas_call x1, Pallas kernels, per_device(): pl.pallas_call(functools.partial(begin_kernel, depth, plane, block, tile_...  38.9 us
    pallas_call x1, Pallas kernels, per_device(): pl.pallas_call(functools.partial(refine_kernel, plane, tile_count, knot_c...  30.1 us
    pallas_call x1, Pallas kernels, per_device(): pl.pallas_call(functools.partial(pair_kernel, rows, cap), out_shape=(f32(...  5.46 us
    unnamed x13, local copies, waits for them, and re-layouts  2.11 us
    pallas_call x1, Pallas kernels, per_device(): pl.pallas_call(functools.partial(warp_kernel, plane, knots), out_shape=f3...  2 us

profile of v5, /device:TPU:0, one launch (start us, length us, event | category | flops | bytes accessed | tf_op | source)
XLA Modules:
  0.0 80.5 jit_solution(6280745176496628974)
XLA Ops:
  0.6 0.8 copy.11.table
  1.4 0.0 copy-start.4
  1.4 0.7 copy-done.4
  2.1 0.0 copy-start.5
  2.1 0.7 copy-done.5
  2.7 0.0 copy-start
  2.7 0.0 copy-start.1
  2.7 38.9 %begin.1 = (f32[384,8,128]{2,1,0:T(8,128)S(1)}, f32[512,128]{1,0:T(8,128)S(1)}, f32[512,128]{1,0:T(8,128)S(1)}, f32[512,8,128]{2,1,0:T(8,128)S(1)}, f32[512,8,12...) custom-call(s32[1,2]{1,0:T(1,128)S(1)} %copy-done.4, ...), custom_call_target="tpu_custom_call" | custom-call | tf_op jit(solution)/shard_map/begin/pallas_call | solution.py:761
  41.7 0.0 copy-done
  41.7 0.0 copy-done.1
  41.7 0.0 copy-start.2
  41.7 0.0 copy-start.3
  41.7 5.5 %pairs.1 = (f32[24,72,128]{2,1,0:T(8,128)S(1)}, f32[24,72,128]{2,1,0:T(8,128)S(1)}) custom-call(s32[1,3,8,5]{3,2,1,0:T(8,128)S(1)} %copy.11.table, f32[512,8,128]{2,1,0:T(8,128)S(1)} %bitcast.10, f32[512,8,128]{2,1,0:T(8,128)S(1)} %bitcast.13, f32[512,8,128]{2,1,0:T(8,128)S(1)} %get-tuple-element.20.below, f32[512,8,128]{2,1,0:T(8,128)S(1)} %get-tuple-element.21.above), custom_call_target="tpu_custom_call" | custom-call | tf_op jit(solution)/shard_map/pairs/pallas_call | solution.py:802
  47.8 0.0 copy-done.2
  47.8 0.0 copy-done.3
  47.8 30.1 %refine.1 = (f32[136,128]{1,0:T(8,128)S(1)}, f32[8,64]{1,0:T(8,128)S(1)}) custom-call(s32[1,2]{1,0:T(1,128)S(1)} %copy-done.4, s32[1,3,8,5]{3,2,1,0:T(8,128)S(1)} %copy.11.table, s32[1]{0:T(128)S(6)} %copy.12.rigid, f32[384,8,128]{2,1,0:T(8,128)S(1)} %get-tuple-element.17.basis, f32[512,128]{1,0:T(8,128)S(1)} %get-tuple-element.18.weight, ...), custom_call_target="tpu_custom_call" | custom-call | tf_op jit(solution)/shard_map/refine/pallas_call | solution.py:813
  78.0 2.0 %warp.1 = f32[512,8,128]{2,1,0:T(8,128)} custom-call(s32[1]{0:T(128)S(6)} %copy.12.rigid, f32[136,128]{1,0:T(8,128)S(1)} %get-tuple-element.31.local, f32[384,8,128]{2,1,0:T(8,128)S(1)} %get-tuple-element.17.basis, f32[512,8,128]{2,1,0:T(8,128)S(1)} %bitcast.11, f32[512,8,128]{2,1,0:T(8,128)S(1)} %bitcast.14), custom_call_target="tpu_custom_call" | custom-call | tf_op jit(solution)/shard_map/warp/pallas_call | solution.py:840
  80.0 0.5 slice.3
Async XLA Ops:
  1.4 0.7 copy-start.4
  2.1 0.7 copy-start.5
  2.7 38.9 %copy-start = (f32[1,8,65536]{2,1,0:T(8,128)S(1)}, f32[1,8,65536]{2,1,0:T(8,128)}, u32[]{:S(2)}) copy-start(f32[1,8,65536]{2,1,0:T(8,128)} %param.7) | copy-start | bytes 6291460
  2.7 38.9 %copy-start.1 = (f32[1,8,65536]{2,1,0:T(8,128)S(1)}, f32[1,8,65536]{2,1,0:T(8,128)}, u32[]{:S(2)}) copy-start(f32[1,8,65536]{2,1,0:T(8,128)} %param.8) | copy-start | bytes 6291460
  41.7 6.1 %copy-start.2 = (f32[24,63,8,128]{3,2,1,0:T(8,128)S(1)}, f32[24,63,8,128]{3,2,1,0:T(8,128)}, u32[]{:S(2)}) copy-start(f32[24,63,8,128]{3,2,1,0:T(8,128)} %get-tuple-element.24.shapes) | copy-start | bytes 18579460
  41.7 6.1 %copy-start.3 = (f32[64,64]{1,0:T(8,128)S(1)}, f32[64,64]{1,0:T(8,128)}, u32[]{:S(2)}) copy-start(f32[64,64]{1,0:T(8,128)} %constant.2.clone.penalty) | copy-start | bytes 49156
